TPU v7x, 256 devices: a whole 4x4x8 slice. The times are simulated.
256 devices in a mesh: mic: 4 (over y_lo, core), tm: 64 (over y_hi, z, x).
Axes of the slice: x: 4, y: 4 (y_hi: 2, y_lo: 2; y = y_hi * 2 + y_lo), z: 8, core: 2. Of those that a mesh axis runs over, the one named last changes fastest.
Arguments:
- frames: bfloat16 [8, 8192, 512], P('mic', 'tm'), may hold values from -6 to 6
- cotangent: bfloat16 [8, 8192, 512], P('mic', 'tm'), may hold values from -6 to 6
- kernel: float32 [31, 512], replicated, may hold values from -1 to 1
- w_query: bfloat16 [512, 512], replicated, may hold values from -0.25 to 0.25
- w_key: bfloat16 [512, 512], replicated, may hold values from -0.25 to 0.25
- w_value: bfloat16 [512, 512], replicated, may hold values from -0.25 to 0.25
- w_out: bfloat16 [512, 512], replicated, may hold values from -0.25 to 0.25
Outputs:
- layer_out: bfloat16 [8, 8192, 512], P('mic', 'tm')
- frame_grad: bfloat16 [8, 8192, 512], P('mic', 'tm')
- kernel_grad: float32 [31, 512], replicated
- query_grad: float32 [512, 512], replicated
- key_grad: float32 [512, 512], replicated
- value_grad: float32 [512, 512], replicated
- out_grad: float32 [512, 512], replicated
All inputs are finite; a program needn't handle non-finite values.
Results may differ from a plain program's by a relative error of at most 0.013.
Values may be sent and summed in bfloat16 or wider, within the bound.
A program may use at most 128 MiB of HBM per device.

v0:
```python
import math

import jax
import jax.numpy as jnp
from jax import lax
from jax.sharding import PartitionSpec as P

HEADS = 8


def extended(array, sides, width):
    for axis, dim in sides:
        size, length = (lax.axis_size(axis), array.shape[dim])
        up = [(i, (i + 1) % size) for i in range(size - 1)]
        down = [(j, i) for i, j in up]
        last = lax.slice_in_dim(array, length - width, length, axis=dim)
        first = lax.slice_in_dim(array, 0, width, axis=dim)
        before = lax.ppermute(last, axis, up)
        after = lax.ppermute(first, axis, down)
        array = jnp.concatenate([before, array, after], axis=dim)
    return array


def depthwise(padded, kernel, length):
    summed = jnp.zeros((padded.shape[0], length, padded.shape[2]), jnp.float32)
    for offset in range(kernel.shape[0]):
        summed = (
            summed + padded[:, offset : offset + length, :].astype(jnp.float32) * kernel[offset]
        )
    return summed


def transposed(padded, kernel, length):
    reach = kernel.shape[0] - 1
    summed = jnp.zeros((padded.shape[0], length, padded.shape[2]), jnp.float32)
    for offset in range(kernel.shape[0]):
        start = reach - offset
        summed = summed + padded[:, start : start + length, :] * kernel[offset]
    return summed


def kernel_terms(padded, gradient, taps):
    length = gradient.shape[1]
    rows_out = []
    for offset in range(taps):
        rows_out.append(
            jnp.sum(
                padded[:, offset : offset + length, :].astype(jnp.float32) * gradient, axis=(0, 1)
            )
        )
    return jnp.stack(rows_out)


def split_heads(rows, head_count):
    first, length, width = rows.shape
    return rows.astype(jnp.float32).reshape(first, length, head_count, width // head_count)


def attend(queries, key_rows, value_rows, head_count):
    first, length, width = queries.shape
    factor = 1.0 / math.sqrt(width // head_count)
    query_heads = split_heads(queries, head_count)
    key_heads = split_heads(key_rows, head_count)
    value_heads = split_heads(value_rows, head_count)
    scores = jnp.einsum("athe,bthe->abth", query_heads, key_heads) * factor
    weights = jnp.exp(scores)
    weights = weights / jnp.sum(weights, axis=1, keepdims=True)
    mixed = jnp.einsum("abth,bthe->athe", weights, value_heads).reshape(first, length, width)
    return (mixed, weights)


def attend_back(queries, key_rows, value_rows, weights, upstream, head_count):
    first, length, width = queries.shape
    others = key_rows.shape[0]
    factor = 1.0 / math.sqrt(width // head_count)
    query_heads = split_heads(queries, head_count)
    key_heads = split_heads(key_rows, head_count)
    value_heads = split_heads(value_rows, head_count)
    up_heads = split_heads(upstream, head_count)
    products = jnp.einsum("athe,bthe->abth", up_heads, value_heads)
    inner = weights * (products - jnp.sum(weights * products, axis=1, keepdims=True)) * factor
    dquery = jnp.einsum("abth,bthe->athe", inner, key_heads).reshape(first, length, width)
    key_terms = jnp.einsum("abth,athe->bthe", inner, query_heads).reshape(others, length, width)
    value_terms = jnp.einsum("abth,athe->bthe", weights, up_heads).reshape(others, length, width)
    return (dquery, key_terms, value_terms)


def project(inputs, matrix):
    width = inputs.shape[-1]
    return jnp.dot(inputs.reshape(-1, width), matrix, preferred_element_type=jnp.float32).reshape(
        inputs.shape[:-1] + (matrix.shape[1],)
    )


def outer(left, right):
    width = left.shape[-1]
    return jnp.dot(
        left.reshape(-1, width).T,
        right.reshape(-1, right.shape[-1]),
        preferred_element_type=jnp.float32,
    )


def shards(frames, cotangent, kernel, w_query, w_key, w_value, w_out):
    reach = kernel.shape[0] // 2
    length = frames.shape[1]
    count = frames.shape[0]
    padded = extended(frames, (("tm", 1),), reach)
    conv = depthwise(padded, kernel, length)
    acted = jax.nn.silu(conv).astype(jnp.bfloat16)
    queries = project(acted, w_query).astype(jnp.bfloat16)
    key_rows = project(acted, w_key).astype(jnp.bfloat16)
    value_rows = project(acted, w_value).astype(jnp.bfloat16)
    key_all, value_all = (
        lax.all_gather(key_rows, "mic", axis=0, tiled=True),
        lax.all_gather(value_rows, "mic", axis=0, tiled=True),
    )
    mixed, weights = attend(queries, key_all, value_all, HEADS)
    mixed = mixed.astype(jnp.bfloat16)
    upstream = project(cotangent, w_out.T).astype(jnp.bfloat16)
    dquery, key_terms, value_terms = attend_back(
        queries, key_all, value_all, weights, upstream, HEADS
    )
    key_sum, value_sum = (
        lax.psum_scatter(key_terms, "mic", scatter_dimension=0, tiled=True),
        lax.psum_scatter(value_terms, "mic", scatter_dimension=0, tiled=True),
    )
    layer_out = (frames.astype(jnp.float32) + project(mixed, w_out)).astype(jnp.bfloat16)
    out_term = outer(mixed, cotangent)
    dquery = dquery.astype(jnp.bfloat16)
    dkey = key_sum.astype(jnp.bfloat16)
    dvalue = value_sum.astype(jnp.bfloat16)
    query_term = outer(acted, dquery)
    key_term = outer(acted, dkey)
    value_term = outer(acted, dvalue)
    dacted = project(dquery, w_query.T) + project(dkey, w_key.T) + project(dvalue, w_value.T)
    sig = jax.nn.sigmoid(conv)
    dconv = dacted * sig * (1.0 + conv * (1.0 - sig))
    grad_pad = extended(dconv.astype(jnp.bfloat16), (("tm", 1),), reach).astype(dconv.dtype)
    frame_grad = (cotangent.astype(jnp.float32) + transposed(grad_pad, kernel, length)).astype(
        jnp.bfloat16
    )
    tap_term = kernel_terms(padded, dconv, kernel.shape[0])
    norm_factor = 1.0 / math.sqrt(lax.axis_size("mic") * count * lax.axis_size("tm") * length)
    summed = lax.psum((tap_term, query_term, key_term, value_term, out_term), ("mic", "tm"))
    kernel_grad = summed[0] * norm_factor
    query_grad = summed[1] * norm_factor
    key_grad = summed[2] * norm_factor
    value_grad = summed[3] * norm_factor
    out_grad = summed[4] * norm_factor
    return (layer_out, frame_grad, kernel_grad, query_grad, key_grad, value_grad, out_grad)


def solution(mesh):
    in_specs = (P("mic", "tm", None), P("mic", "tm", None), P(), P(), P(), P(), P())
    out_specs = (P("mic", "tm", None), P("mic", "tm", None), P(), P(), P(), P(), P())
    return jax.shard_map(shards, mesh=mesh, in_specs=in_specs, out_specs=out_specs, check_vma=False)
```

profile of v0, /device:TPU:1, one launch (start us, length us, event | category | flops | bytes accessed | tf_op | source)
XLA Modules:
  0.0 460.2 jit_solution(15182263519560955527)
XLA Ops:
  9.4 4.6 collective-permute-start
  17.4 6.1 %multiply_convert_fusion = (bf16[2,128,512]{2,1,0:T(8,128)(2,1)S(1)}, f32[2,128,512]{2,1,0:T(8,128)}) fusion(f32[512]{0:T(512)S(1)} %bitcast.166, bf16[2,143,512]{2,1,0:T(8,128)(2,1)S(1)} %constant_dynamic-update-slice_fusion, f32[512]{0:T(512)S(1)} %bitcast.168, f32[512]{0:T(512)S(1)} %bitcast.172, f32[512]{0:T(512)S(1)} %bitcast.174, ...), kind=kLoop, calls=%fused_computation.241 | loop fusion | flops 18612224 | bytes 5074944 | tf_op jit(solution)/shard_map/convert_element_type | solution.py:110
  29.0 26.8 %all-gather.3.cloned.1.call-done = bf16[8,128,512]{2,1,0:T(8,128)(2,1)} async-done(((bf16[2,128,512]{2,1,0:T(8,128)(2,1)}), bf16[8,128,512]{2,1,0:T(8,128)(2,1)}) %all-gather.3.cloned.1.call-update) | async-done | bytes 1048592 | tf_op jit(solution)/shard_map/all_gather | solution.py:116
  55.8 1.6 copy.52
  57.4 3.8 copy.57
  61.2 21.2 %all-gather.5.cloned.1.call-done = bf16[8,128,512]{2,1,0:T(8,128)(2,1)} async-done(((bf16[2,128,512]{2,1,0:T(8,128)(2,1)}), bf16[8,128,512]{2,1,0:T(8,128)(2,1)}) %all-gather.5.cloned.1.call-update) | async-done | bytes 1048592 | tf_op jit(solution)/shard_map/all_gather | solution.py:115
  84.1 3.7 copy.55
  87.9 4.0 convolution_bitcast_fusion.6
  91.9 5.1 %multiply_reduce_fusion = (f32[2,128,8]{0,2,1:T(8,128)}, f32[2,8,128,8]{1,0,3,2:T(2,128)}) fusion(f32[2,8,128,8]{1,0,3,2:T(2,128)} %convolution_bitcast_fusion.6, bf16[8,128,8,64]{3,0,2,1:T(8,128)(2,1)S(1)} %copy-done.4, bf16[2,128,8,64]{3,0,2,1:T(2,128)(2,1)} %copy.56), kind=kOutput, calls=%fused_computation.39 | convolution fusion | flops 2162695 | bytes 1449984 | tf_op jit(solution)/shard_map/div | solution.py:67
  96.9 5.7 %convolution_bitcast_fusion.1 = f32[8,128,8,64]{3,0,2,1:T(8,128)} fusion(bf16[2,128,8,64]{3,0,2,1:T(2,128)(2,1)} %copy.56, f32[2,8,128,8]{1,0,3,2:T(2,128)} %get-tuple-element.81, f32[2,8,128,8]{1,0,3,2:T(2,128)} %convolution_bitcast_fusion.6, f32[2,128,8]{0,2,1:T(8,128)} %get-tuple-element.80), kind=kOutput, calls=%fused_computation.1 | convolution fusion | flops 2146304 | bytes 2498560 | tf_op jit(solution)/shard_map/abth,athe->bthe/dot_general | solution.py:83
  102.6 4.8 %copy.67 = f32[8,128,8,64]{1,3,2,0:T(8,128)} copy(f32[8,128,8,64]{3,0,2,1:T(8,128)} %convolution_bitcast_fusion.1) | data formatting | bytes 4194304 | tf_op jit(solution)/shard_map/abth,athe->bthe/transpose | solution.py:83
  108.8 2.9 convolution_bitcast_fusion
  111.7 4.8 %copy.70 = f32[8,128,8,64]{1,3,2,0:T(8,128)} copy(f32[8,128,8,64]{3,0,2,1:T(8,128)} %convolution_bitcast_fusion) | data formatting | bytes 4194304 | tf_op jit(solution)/shard_map/abth,athe->bthe/transpose | solution.py:84
  118.0 3.2 fusion.2
  122.6 3.9 fusion.3
  131.0 8.2 %reduce-scatter.3.cloned.1.call-done = f32[2,128,512]{1,2,0:T(8,128)} async-done(((f32[8,128,512]{1,2,0:T(8,128)}), f32[2,128,512]{1,2,0:T(8,128)}) %reduce-scatter.3.cloned.1.call-update) | async-done | bytes 524304 | tf_op jit(solution)/shard_map/reduce_scatter | solution.py:125
  139.2 2.4 convolution_bitcast_fusion.4
  141.5 32.0 %reduce-scatter.5.cloned.1.call-done = f32[2,128,512]{1,2,0:T(8,128)} async-done(((f32[8,128,512]{1,2,0:T(8,128)}), f32[2,128,512]{1,2,0:T(8,128)}) %reduce-scatter.5.cloned.1.call-update) | async-done | bytes 524304 | tf_op jit(solution)/shard_map/reduce_scatter | solution.py:126
  173.5 2.4 convolution_bitcast_fusion.3
  181.3 4.0 collective-permute-start.2
  186.6 83.0 %psum.35 = f32[31,512]{1,0:T(8,128)S(1)} all-reduce(f32[31,512]{1,0:T(8,128)S(1)} %stack.127), channel_id=1, replica_groups=mesh['mic'=4,'tm'=64] {'mic','tm'}, use_global_device_ids=true, to_apply=%region_35.36 | all-reduce | flops 15872 | bytes 126976 | tf_op jit(solution)/shard_map/psum | solution.py:145
  270.5 2.8 fusion.70
  273.2 175.6 %all-reduce.3.cloned.1.call-done = (f32[512,512]{1,0:T(8,128)}, f32[512,512]{1,0:T(8,128)}, f32[512,512]{1,0:T(8,128)}, f32[512,512]{1,0:T(8,128)}) async-done(((f32[512,512]{1,0:T(8,128)}, f32[512,512]{1,0:T(8,128)}, f32[512,512]{1,0:T(8,128)}, f32[512,512]{1,0:T(8,128)}), (f32[512,512]{1,0:T(8,128)}, f32[512,512]{1,0:T(8,128)}, f32[512,512]{1,0:T(8,128)}, ...) | async-done | bytes 4194320 | tf_op jit(solution)/shard_map/psum | solution.py:145
  448.9 3.2 broadcast_multiply_fusion.2
  (125 shorter events, 30.2 us)
Async XLA Ops:
  7.2 16.3 %copy-start = (bf16[512,512]{1,0:T(8,128)(2,1)S(1)}, bf16[512,512]{1,0:T(8,128)(2,1)}, u32[]{:S(2)}) copy-start(bf16[512,512]{1,0:T(8,128)(2,1)} %param.12) | copy-start | bytes 1572868
  7.2 48.6 %all-gather.3.cloned.1.call-start = ((), (), s32[]{:S(2)}) async-start(), calls=%async_computation.2 | async-start | bytes 1310720 | tf_op jit(solution)/shard_map/all_gather | solution.py:116
  8.1 9.2 %collective-permute-start.1 = (bf16[2,15,512]{2,1,0:T(8,128)(2,1)S(1)}, bf16[2,15,512]{2,1,0:T(8,128)(2,1)S(1)}, u32[]{:S(2)}, u32[]{:S(2)}) collective-permute-start(bf16[2,15,512]{2,1,0:T(8,128)(2,1)S(1)} %get-tuple-element.48), channel_id=1, source_target_pairs={{1,0},{2,1},{3,2},{4,3},{5,4},{6,5},{7,6},{8,7},{9,8},{10,9},{11,1... | collective-permute-start | bytes 92168 | tf_op jit(solution)/shard_map/ppermute | solution.py:19
  9.4 7.9 %collective-permute-start = (bf16[2,15,512]{2,1,0:T(8,128)(2,1)S(1)}, bf16[2,15,512]{2,1,0:T(8,128)(2,1)S(1)}, u32[]{:S(2)}, u32[]{:S(2)}) collective-permute-start(bf16[2,15,512]{2,1,0:T(8,128)(2,1)S(1)} %get-tuple-element.47), channel_id=1, source_target_pairs={{0,1},{1,2},{2,3},{3,4},{4,5},{5,6},{6,7},{7,8},{8,9},{9,10},{10,1... | collective-permute-start | bytes 92168 | tf_op jit(solution)/shard_map/ppermute | solution.py:18
  17.4 7.2 %copy-start.10 = (bf16[512,512]{1,0:T(8,128)(2,1)S(1)}, bf16[512,512]{1,0:T(8,128)(2,1)}, u32[]{:S(2)}) copy-start(bf16[512,512]{1,0:T(8,128)(2,1)} %param.11) | copy-start | bytes 1572868
  24.5 58.0 %all-gather.5.cloned.1.call-start = ((), (), s32[]{:S(2)}) async-start(), calls=%async_computation.3 | async-start | bytes 1310720 | tf_op jit(solution)/shard_map/all_gather | solution.py:115
  25.6 113.6 %reduce-scatter.3.cloned.1.call-start = ((), (), s32[]{:S(2)}) async-start(), calls=%async_computation.4 | async-start | bytes 2621440 | tf_op jit(solution)/shard_map/reduce_scatter | solution.py:125
  87.8 4.0 copy-start.4
  107.4 66.1 %reduce-scatter.5.cloned.1.call-start = ((), (), s32[]{:S(2)}) async-start(), calls=%async_computation.5 | async-start | bytes 2621440 | tf_op jit(solution)/shard_map/reduce_scatter | solution.py:126
  116.5 332.4 %all-reduce.3.cloned.1.call-start = ((), (), s32[]{:S(2)}) async-start(), calls=%async_computation.6 | async-start | bytes 8388608 | tf_op jit(solution)/shard_map/psum | solution.py:145
  127.0 3.6 copy-start.8
  179.9 90.5 %copy-start.19 = (f32[1,512]{1,0:T(1,128)S(1)}, f32[1,512]{1,0:T(1,128)}, u32[]{:S(2)}) copy-start(f32[1,512]{1,0:T(1,128)} %copy-done.18) | copy-start | bytes 6148
  179.9 90.5 %copy-start.21 = (f32[1,512]{1,0:T(1,128)S(1)}, f32[1,512]{1,0:T(1,128)}, u32[]{:S(2)}) copy-start(f32[1,512]{1,0:T(1,128)} %copy-done.20) | copy-start | bytes 6148
  179.9 90.5 %copy-start.23 = (f32[1,512]{1,0:T(1,128)S(1)}, f32[1,512]{1,0:T(1,128)}, u32[]{:S(2)}) copy-start(f32[1,512]{1,0:T(1,128)} %copy-done.22) | copy-start | bytes 6148
  179.9 90.5 %copy-start.25 = (f32[1,512]{1,0:T(1,128)S(1)}, f32[1,512]{1,0:T(1,128)}, u32[]{:S(2)}) copy-start(f32[1,512]{1,0:T(1,128)} %copy-done.24) | copy-start | bytes 6148
  179.9 90.5 %copy-start.27 = (f32[1,512]{1,0:T(1,128)S(1)}, f32[1,512]{1,0:T(1,128)}, u32[]{:S(2)}) copy-start(f32[1,512]{1,0:T(1,128)} %copy-done.26) | copy-start | bytes 6148
  179.9 90.5 %copy-start.29 = (f32[1,512]{1,0:T(1,128)S(1)}, f32[1,512]{1,0:T(1,128)}, u32[]{:S(2)}) copy-start(f32[1,512]{1,0:T(1,128)} %copy-done.28) | copy-start | bytes 6148
  180.0 90.5 %copy-start.31 = (f32[1,512]{1,0:T(1,128)S(1)}, f32[1,512]{1,0:T(1,128)}, u32[]{:S(2)}) copy-start(f32[1,512]{1,0:T(1,128)} %copy-done.30) | copy-start | bytes 6148
  180.0 90.5 %copy-start.33 = (f32[1,512]{1,0:T(1,128)S(1)}, f32[1,512]{1,0:T(1,128)}, u32[]{:S(2)}) copy-start(f32[1,512]{1,0:T(1,128)} %copy-done.32) | copy-start | bytes 6148
  180.0 90.5 %copy-start.35 = (f32[1,512]{1,0:T(1,128)S(1)}, f32[1,512]{1,0:T(1,128)}, u32[]{:S(2)}) copy-start(f32[1,512]{1,0:T(1,128)} %copy-done.34) | copy-start | bytes 6148
  180.0 90.5 %copy-start.37 = (f32[1,512]{1,0:T(1,128)S(1)}, f32[1,512]{1,0:T(1,128)}, u32[]{:S(2)}) copy-start(f32[1,512]{1,0:T(1,128)} %copy-done.36) | copy-start | bytes 6148
  180.0 90.5 %copy-start.39 = (f32[1,512]{1,0:T(1,128)S(1)}, f32[1,512]{1,0:T(1,128)}, u32[]{:S(2)}) copy-start(f32[1,512]{1,0:T(1,128)} %copy-done.38) | copy-start | bytes 6148
  180.0 90.2 %collective-permute-start.3 = (bf16[2,15,512]{2,1,0:T(8,128)(2,1)S(1)}, bf16[2,15,512]{2,1,0:T(8,128)(2,1)S(1)}, u32[]{:S(2)}, u32[]{:S(2)}) collective-permute-start(bf16[2,15,512]{2,1,0:T(8,128)(2,1)S(1)} %get-tuple-element.46), channel_id=1, source_target_pairs={{1,0},{2,1},{3,2},{4,3},{5,4},{6,5},{7,6},{8,7},{9,8},{10,9},{11,1... | collective-permute-start | bytes 92168 | tf_op jit(solution)/shard_map/ppermute | solution.py:19
  181.3 88.9 %collective-permute-start.2 = (bf16[2,15,512]{2,1,0:T(8,128)(2,1)S(1)}, bf16[2,15,512]{2,1,0:T(8,128)(2,1)S(1)}, u32[]{:S(2)}, u32[]{:S(2)}) collective-permute-start(bf16[2,15,512]{2,1,0:T(8,128)(2,1)S(1)} %get-tuple-element.45), channel_id=1, source_target_pairs={{0,1},{1,2},{2,3},{3,4},{4,5},{5,6},{6,7},{7,8},{8,9},{9,10},{10,1... | collective-permute-start | bytes 92168 | tf_op jit(solution)/shard_map/ppermute | solution.py:18
  (25 other events, 41.3 us)
Sparse Core Ops, SparseCore 0:
  24.6 31.1 all-gather.2
  58.2 24.2 all-gather.4
  107.5 31.6 reduce-scatter.2
  141.7 31.7 reduce-scatter.4
  179.8 269.0 all-reduce.2
where the time goes:
time: 462 us; the launch traced here: 460 us
  waiting for transfers between devices  264 us (57%)
  blocking collectives  83 us (18%)
  matrix products  38.1 us (8%)
  local copies, waits for them, and re-layouts  33.6 us (7%)
  other arithmetic  15.5 us (3%)
  between operations  14.4 us (3%)
  starting transfers between devices  11.8 us (3%)
    psum x1, waiting for transfers between devices, shards(): lax.psum((tap_term, query_term, key_term, value_term, out_term), ('mic',...  176 us
    psum x1, blocking collectives, shards(): lax.psum((tap_term, query_term, key_term, value_term, out_term), ('mic',...  83 us
    reduce_scatter x1, waiting for transfers between devices, shards(): lax.psum_scatter(value_terms, 'mic', scatter_dimension=0, tiled=True)  32 us
    all_gather x1, waiting for transfers between devices, shards(): lax.all_gather(value_rows, 'mic', axis=0, tiled=True)  26.8 us
    all_gather x1, waiting for transfers between devices, shards(): lax.all_gather(key_rows, 'mic', axis=0, tiled=True)  21.2 us
    reshape x4, local copies, waits for them, and re-layouts, split_heads(): rows.astype(jnp.float32)  9.76 us
  transfers between devices with their start and end apart: 9, of which 5 were waited for; matrix products, arithmetic and copies ran while one was open for 9% of the time, Pallas kernels for 0%

commit v1 on v0

--- a/solution.py
+++ b/solution.py
@@ -1,11 +1,387 @@
+import functools
 import math
 
 import jax
 import jax.numpy as jnp
 from jax import lax
+from jax.experimental import pallas as pl
+from jax.experimental.pallas import tpu as pltpu
 from jax.sharding import PartitionSpec as P
 
 HEADS = 8
+NX, NY, NZ = 4, 4, 8
+MESH = pl.DeviceIdType.MESH
+
+
+class Place:
+    def __init__(self):
+        mic = lax.axis_index("mic")
+        tm = lax.axis_index("tm")
+        self.core = lax.rem(mic, 2)
+        self.x = lax.rem(tm, NX)
+        self.z = lax.rem(lax.div(tm, NX), NZ)
+        self.y = lax.div(tm, NX * NZ) * 2 + lax.div(mic, 2)
+
+    def device(self, x=None, y=None, z=None, core=None):
+        x = self.x if x is None else x
+        y = self.y if y is None else y
+        z = self.z if z is None else z
+        core = self.core if core is None else core
+        mic = lax.rem(y, 2) * 2 + core
+        tm = lax.div(y, 2) * (NX * NZ) + z * NX + x
+        return (mic, tm)
+
+    def along(self, axis, step):
+        size = {"x": NX, "y": NY, "z": NZ, "core": 2}[axis]
+        index = lax.rem(getattr(self, axis) + step, size)
+        return index, self.device(**{axis: index})
+
+
+def rows_at(start, count):
+    return pl.ds(pl.multiple_of(start, count), count)
+
+
+def send(src, dst, send_sem, recv_sem, device):
+    copy = pltpu.make_async_remote_copy(
+        src_ref=src,
+        dst_ref=dst,
+        send_sem=send_sem,
+        recv_sem=recv_sem,
+        device_id=device,
+        device_id_type=MESH,
+    )
+    copy.start()
+    return copy
+
+
+def greet(peers):
+    barrier = pltpu.get_barrier_semaphore()
+    for peer in peers:
+        pl.semaphore_signal(barrier, inc=1, device_id=peer, device_id_type=MESH)
+    pl.semaphore_wait(barrier, len(peers))
+
+
+SIZES = {"x": NX, "y": NY, "z": NZ, "core": 2}
+HALF, STREAM, FIRST, SECOND, TILE = 4096, 2048, 512, 128, 16
+ORDERS = (("x", "y", "z"), ("y", "x", "z"))
+
+
+def f32(value):
+    return value.astype(jnp.float32)
+
+
+def sum_kernel(
+    scale,
+    q_ref,
+    k_ref,
+    v_ref,
+    o_ref,
+    tap_ref,
+    out_ref,
+    tap_out,
+    mine,
+    full,
+    core_rx,
+    rx1,
+    rx2,
+    rx3,
+    tap0,
+    tap_zrx,
+    tap_rx,
+    tap_full,
+    core_s,
+    core_r,
+    s1,
+    r1,
+    s2,
+    r2,
+    s3,
+    r3,
+    gs,
+    gr,
+    gcs,
+    gcr,
+    ts,
+    tr,
+    tgs,
+    tgr,
+):
+    here = Place()
+    peers = []
+    for axis in ("core", "x", "y", "z"):
+        for step in range(1, SIZES[axis]):
+            peers.append(here.along(axis, step)[1])
+    greet(peers)
+    sent = []
+    own = here.core * HALF
+    other, sibling = here.along("core", 1)
+    for g, ref in enumerate((q_ref, k_ref, v_ref, o_ref)):
+        for block in range(4):
+            at = (g * 4 + block) * 512
+            mine[at : at + 512, :] = ref[:, block * 128 : (block + 1) * 128].astype(jnp.bfloat16)
+    for s in range(2):
+        sent.append(
+            send(
+                mine.at[rows_at(other * HALF + s * STREAM, STREAM)],
+                core_rx.at[s],
+                core_s.at[s],
+                core_r.at[s],
+                sibling,
+            )
+        )
+    core_copies = sent[:]
+    for block in range(4):
+        tap0[block * 32 : block * 32 + 32, :] = tap_ref[:, block * 128 : (block + 1) * 128]
+    tap_copies = []
+    for step in range(1, NZ):
+        index, peer = here.along("z", step)
+        tap_copies.append(
+            send(
+                tap0.at[rows_at(index * 16, 16)],
+                tap_zrx.at[step - 1],
+                ts.at[step - 1],
+                tr.at[step - 1],
+                peer,
+            )
+        )
+    sent += tap_copies
+
+    first = []
+    for s in range(2):
+        core_copies[s].wait_recv()
+        part = rows_at(own + s * STREAM, STREAM)
+        mine[part, :] = (f32(mine[part, :]) + f32(core_rx[s])).astype(jnp.bfloat16)
+        axis = ORDERS[s][0]
+        copies = []
+        for step in range(1, SIZES[axis]):
+            index, peer = here.along(axis, step)
+            copies.append(
+                send(
+                    mine.at[rows_at(own + s * STREAM + index * FIRST, FIRST)],
+                    rx1.at[s, step - 1],
+                    s1.at[s, step - 1],
+                    r1.at[s, step - 1],
+                    peer,
+                )
+            )
+        first.append(copies)
+        sent += copies
+
+    total = tap0[rows_at(here.z * 16, 16), :]
+    for step in range(1, NZ):
+        tap_copies[step - 1].wait_recv()
+        total = total + tap_zrx[step - 1]
+
+    def tap_axis(tile, axis, base):
+        slot = base + getattr(here, axis)
+        tap_rx[slot] = tile
+        copies = []
+        for step in range(1, SIZES[axis]):
+            copies.append(
+                send(
+                    tap_rx.at[slot],
+                    tap_rx.at[slot],
+                    ts.at[NZ - 1 + base + step - 1],
+                    tr.at[NZ - 1 + base + step - 1],
+                    here.along(axis, step)[1],
+                )
+            )
+        return copies
+
+    def tap_sum(copies, base):
+        for copy in copies:
+            copy.wait_recv()
+        total = tap_rx[base]
+        for index in range(len(copies)):
+            total = total + tap_rx[base + 1 + index]
+        return total
+
+    tap_x = tap_axis(total, "x", 0)
+    sent += tap_x
+
+    second = []
+    for s in range(2):
+        axis, axis2, _ = ORDERS[s]
+        place = own + s * STREAM + getattr(here, axis) * FIRST
+        for copy in first[s]:
+            copy.wait_recv()
+        part = rows_at(place, FIRST)
+        total = f32(mine[part, :])
+        for step in range(SIZES[axis] - 1):
+            total = total + f32(rx1[s, step])
+        mine[part, :] = total.astype(jnp.bfloat16)
+        copies = []
+        for step in range(1, SIZES[axis2]):
+            index, peer = here.along(axis2, step)
+            copies.append(
+                send(
+                    mine.at[rows_at(place + index * SECOND, SECOND)],
+                    rx2.at[s, step - 1],
+                    s2.at[s, step - 1],
+                    r2.at[s, step - 1],
+                    peer,
+                )
+            )
+        second.append((place, copies))
+        sent += copies
+
+    tap_y = tap_axis(tap_sum(tap_x, 0), "y", 4)
+    sent += tap_y
+
+    third = []
+    for s in range(2):
+        axis2 = ORDERS[s][1]
+        place, copies = second[s]
+        place = place + getattr(here, axis2) * SECOND
+        for copy in copies:
+            copy.wait_recv()
+        part = rows_at(place, SECOND)
+        total = f32(mine[part, :])
+        for step in range(SIZES[axis2] - 1):
+            total = total + f32(rx2[s, step])
+        mine[part, :] = total.astype(jnp.bfloat16)
+        copies = []
+        for step in range(1, NZ):
+            index, peer = here.along("z", step)
+            copies.append(
+                send(
+                    mine.at[rows_at(place + index * TILE, TILE)],
+                    rx3.at[s, step - 1],
+                    s3.at[s, step - 1],
+                    r3.at[s, step - 1],
+                    peer,
+                )
+            )
+        third.append((place, copies))
+        sent += copies
+
+    tap_c = tap_axis(tap_sum(tap_y, 4), "core", 8)
+    sent += tap_c
+
+    def gather(s, level, axis, place, count):
+        copies = []
+        base = (0, NZ - 1, NZ + 2)[level]
+        part = rows_at(place, count)
+        for step in range(1, SIZES[axis]):
+            copies.append(
+                send(
+                    full.at[part],
+                    full.at[part],
+                    gs.at[s, base + step - 1],
+                    gr.at[s, base + step - 1],
+                    here.along(axis, step)[1],
+                )
+            )
+        return copies
+
+    back = []
+    for s in range(2):
+        place, copies = third[s]
+        for copy in copies:
+            copy.wait_recv()
+        part = rows_at(place + here.z * TILE, TILE)
+        total = f32(mine[part, :])
+        for step in range(NZ - 1):
+            total = total + f32(rx3[s, step])
+        full[part, :] = (total * scale).astype(jnp.bfloat16)
+        copies = gather(s, 0, "z", place + here.z * TILE, TILE)
+        back.append((place, copies))
+        sent += copies
+
+    part = rows_at(here.z * 16, 16)
+    tap_full[part, :] = tap_sum(tap_c, 8) * scale
+    tap_back = []
+    for step in range(1, NZ):
+        tap_back.append(
+            send(
+                tap_full.at[part],
+                tap_full.at[part],
+                tgs.at[step - 1],
+                tgr.at[step - 1],
+                here.along("z", step)[1],
+            )
+        )
+    sent += tap_back
+
+    for level in (1, 2):
+        for s in range(2):
+            place, copies = back[s]
+            for copy in copies:
+                copy.wait_recv()
+            axis = ORDERS[s][2 - level]
+            count = (TILE, SECOND, FIRST)[level]
+            copies = gather(s, level, axis, place, count)
+            back[s] = (place - getattr(here, axis) * count, copies)
+            sent += copies
+    last = []
+    for s in range(2):
+        place, copies = back[s]
+        for copy in copies:
+            copy.wait_recv()
+        part = rows_at(own + s * STREAM, STREAM)
+        copy = send(full.at[part], full.at[part], gcs.at[s], gcr.at[s], sibling)
+        last.append(copy)
+    sent += last
+    for copy in tap_back:
+        copy.wait_recv()
+    for block in range(4):
+        tap_out[:, block * 128 : (block + 1) * 128] = tap_full[block * 32 : block * 32 + 32, :]
+    for copy in last:
+        copy.wait_recv()
+    for g in range(4):
+        for block in range(4):
+            at = (g * 4 + block) * 512
+            out_ref[g, :, block * 128 : (block + 1) * 128] = full[at : at + 512, :]
+    for copy in sent:
+        copy.wait_send()
+
+
+def summed_over_devices(tap_term, query_term, key_term, value_term, out_term, scale):
+    taps, width = tap_term.shape
+    tap_rows = jnp.pad(tap_term, ((0, 32 - taps), (0, 0)))
+    bf16, full32 = jnp.bfloat16, jnp.float32
+    dma = pltpu.SemaphoreType.DMA
+    grads, tap_sum = pl.pallas_call(
+        functools.partial(sum_kernel, scale),
+        out_shape=(
+            jax.ShapeDtypeStruct((4, width, width), bf16),
+            jax.ShapeDtypeStruct((32, width), full32),
+        ),
+        in_specs=[pl.BlockSpec(memory_space=pltpu.VMEM)] * 5,
+        out_specs=[pl.BlockSpec(memory_space=pltpu.VMEM)] * 2,
+        scratch_shapes=[
+            pltpu.VMEM((2 * HALF, 128), bf16),
+            pltpu.VMEM((2 * HALF, 128), bf16),
+            pltpu.VMEM((2, STREAM, 128), bf16),
+            pltpu.VMEM((2, 3, FIRST, 128), bf16),
+            pltpu.VMEM((2, 3, SECOND, 128), bf16),
+            pltpu.VMEM((2, NZ - 1, TILE, 128), bf16),
+            pltpu.VMEM((128, 128), full32),
+            pltpu.VMEM((NZ - 1, 16, 128), full32),
+            pltpu.VMEM((10, 16, 128), full32),
+            pltpu.VMEM((128, 128), full32),
+            dma((2,)),
+            dma((2,)),
+            dma((2, 3)),
+            dma((2, 3)),
+            dma((2, 3)),
+            dma((2, 3)),
+            dma((2, NZ - 1)),
+            dma((2, NZ - 1)),
+            dma((2, NZ + 5)),
+            dma((2, NZ + 5)),
+            dma((2,)),
+            dma((2,)),
+            dma((NZ + 8,)),
+            dma((NZ + 8,)),
+            dma((NZ - 1,)),
+            dma((NZ - 1,)),
+        ],
+        compiler_params=pltpu.CompilerParams(
+            collective_id=0, has_side_effects=True, vmem_limit_bytes=40 * 2**20
+        ),
+    )(query_term, key_term, value_term, out_term, tap_rows)
+    return (tap_sum[:taps],) + tuple(f32(grads[g]) for g in range(4))
 
 
 def extended(array, sides, width):
@@ -142,12 +518,9 @@
     )
     tap_term = kernel_terms(padded, dconv, kernel.shape[0])
     norm_factor = 1.0 / math.sqrt(lax.axis_size("mic") * count * lax.axis_size("tm") * length)
-    summed = lax.psum((tap_term, query_term, key_term, value_term, out_term), ("mic", "tm"))
-    kernel_grad = summed[0] * norm_factor
-    query_grad = summed[1] * norm_factor
-    key_grad = summed[2] * norm_factor
-    value_grad = summed[3] * norm_factor
-    out_grad = summed[4] * norm_factor
+    kernel_grad, query_grad, key_grad, value_grad, out_grad = summed_over_devices(
+        tap_term, query_term, key_term, value_term, out_term, norm_factor
+    )
     return (layer_out, frame_grad, kernel_grad, query_grad, key_grad, value_grad, out_grad)
 
 

time: 462 us -> 252 us (0.55)
  waiting for transfers between devices: 264 us -> 87.1 us
  blocking collectives: 83 us -> 0 us
  Pallas kernels: 0 us -> 50.3 us
    psum x1 -> x0, waiting for transfers between devices: 176 us -> none  [shards(): lax.psum((tap_term, query_term, key_term, value_term, out_term), ('mic',...]
    psum x1 -> x0, blocking collectives: 83 us -> none  [shards(): lax.psum((tap_term, query_term, key_term, value_term, out_term), ('mic',...]
    pallas_call x0 -> x1, Pallas kernels: none -> 50.3 us  [summed_over_devices(): pl.pallas_call(functools.partial(sum_kernel, scale), out_shape=(jax.Shape...]
    mul x3 -> x0, other arithmetic: 5.42 us -> none  [the longest x1 3.24 us: shards(): key_grad = summed[2] * norm_factor]
    dot_general x8, matrix products: 5.96 us -> 10.8 us  [project(): jnp.dot(inputs.reshape(-1, width), matrix, preferred_element_type=jnp.flo...]
  transfers between devices with their start and end apart: 9 -> 8, of which waited for: 5 -> 4; matrix products, arithmetic and copies ran while one was open for 9% -> 18% of each run, Pallas kernels for 0% -> 20%
where the time goes in v1:
time: 252 us
  waiting for transfers between devices  87.1 us (35%)
  Pallas kernels  50.3 us (20%)
  matrix products  40.2 us (16%)
  local copies, waits for them, and re-layouts  34.7 us (14%)
  between operations  14.5 us (6%)
  other arithmetic  12.8 us (5%)
  starting transfers between devices  12 us (5%)
    pallas_call x1, Pallas kernels, summed_over_devices(): pl.pallas_call(functools.partial(sum_kernel, scale), out_shape=(jax.Shape...  50.3 us
    reduce_scatter x1, waiting for transfers between devices, shards(): lax.psum_scatter(value_terms, 'mic', scatter_dimension=0, tiled=True)  31.8 us
    all_gather x1, waiting for transfers between devices, shards(): lax.all_gather(value_rows, 'mic', axis=0, tiled=True)  26.7 us
    all_gather x1, waiting for transfers between devices, shards(): lax.all_gather(key_rows, 'mic', axis=0, tiled=True)  21.2 us
    dot_general x8, matrix products, project(): jnp.dot(inputs.reshape(-1, width), matrix, preferred_element_type=jnp.flo...  10.8 us
    reshape x4, local copies, waits for them, and re-layouts, split_heads(): rows.astype(jnp.float32)  9.81 us
    ppermute x2, starting transfers between devices, extended(): before = lax.ppermute(last, axis, up)  8.82 us
    reduce_scatter x1, waiting for transfers between devices, shards(): lax.psum_scatter(key_terms, 'mic', scatter_dimension=0, tiled=True)  7.27 us
  transfers between devices with their start and end apart: 8, of which 4 were waited for; matrix products, arithmetic and copies ran while one was open for 18% of the time, Pallas kernels for 20%

profile of v1, /device:TPU:1, one launch (start us, length us, event | category | flops | bytes accessed | tf_op | source)
XLA Modules:
  0.0 251.6 jit_solution(17612315022106099428)
XLA Ops:
  9.4 4.6 %collective-permute-start = (bf16[2,15,512]{2,1,0:T(8,128)(2,1)S(1)}, bf16[2,15,512]{2,1,0:T(8,128)(2,1)S(1)}, u32[]{:S(2)}, u32[]{:S(2)}) collective-permute-start(bf16[2,15,512]{2,1,0:T(8,128)(2,1)S(1)} %get-tuple-element.51), channel_id=1, source_target_pairs={{0,1},{1,2},{2,3},{3,4},{4,5},{5,6},{6,7},{7,8},{8,9},{9,10},{10,1... | collective-permute-start | bytes 92168 | tf_op jit(solution)/shard_map/ppermute | solution.py:394
  17.3 6.6 %multiply_convert_fusion = (bf16[2,128,512]{2,1,0:T(8,128)(2,1)S(1)}, f32[2,128,512]{2,1,0:T(8,128)}) fusion(f32[512]{0:T(512)S(1)} %bitcast.180, bf16[2,143,512]{2,1,0:T(8,128)(2,1)S(1)} %constant_dynamic-update-slice_fusion, f32[512]{0:T(512)S(1)} %bitcast.182, f32[512]{0:T(512)S(1)} %bitcast.186, f32[512]{0:T(512)S(1)} %bitcast.188, ...), kind=kLoop, calls=%fused_computation.241 | loop fusion | flops 18612224 | bytes 5074944 | tf_op jit(solution)/shard_map/convert_element_type | solution.py:486
  29.6 26.7 %all-gather.3.cloned.1.call-done = bf16[8,128,512]{2,1,0:T(8,128)(2,1)} async-done(((bf16[2,128,512]{2,1,0:T(8,128)(2,1)}), bf16[8,128,512]{2,1,0:T(8,128)(2,1)}) %all-gather.3.cloned.1.call-update) | async-done | bytes 1048592 | tf_op jit(solution)/shard_map/all_gather | solution.py:492
  56.3 1.6 copy.52
  57.9 3.8 %copy.57 = bf16[8,128,8,64]{3,0,2,1:T(8,128)(2,1)} copy(bf16[8,128,8,64]{1,3,2,0:T(8,128)(2,1)S(1)} %bitcast.152) | data formatting | bytes 2097152 | tf_op jit(solution)/shard_map/reshape | solution.py:432
  61.7 21.2 %all-gather.5.cloned.1.call-done = bf16[8,128,512]{2,1,0:T(8,128)(2,1)} async-done(((bf16[2,128,512]{2,1,0:T(8,128)(2,1)}), bf16[8,128,512]{2,1,0:T(8,128)(2,1)}) %all-gather.5.cloned.1.call-update) | async-done | bytes 1048592 | tf_op jit(solution)/shard_map/all_gather | solution.py:491
  84.6 3.7 %copy.55 = bf16[8,128,8,64]{3,0,2,1:T(8,128)(2,1)} copy(bf16[8,128,8,64]{1,3,2,0:T(8,128)(2,1)S(1)} %bitcast.153) | data formatting | bytes 2097152 | tf_op jit(solution)/shard_map/reshape | solution.py:432
  88.3 4.0 %convolution_bitcast_fusion.6 = f32[2,8,128,8]{1,0,3,2:T(2,128)} fusion(bf16[8,128,8,64]{3,0,2,1:T(8,128)(2,1)} %copy.57, bf16[2,128,8,64]{3,0,2,1:T(2,128)(2,1)} %copy.62), kind=kOutput, calls=%fused_computation.20 | convolution fusion | flops 2097152 | bytes 1376256 | tf_op jit(solution)/shard_map/athe,bthe->abth/dot_general | solution.py:456
  92.4 5.1 %multiply_reduce_fusion = (f32[2,128,8]{0,2,1:T(8,128)}, f32[2,8,128,8]{1,0,3,2:T(2,128)}) fusion(f32[2,8,128,8]{1,0,3,2:T(2,128)} %convolution_bitcast_fusion.6, bf16[8,128,8,64]{3,0,2,1:T(8,128)(2,1)S(1)} %copy-done.8, bf16[2,128,8,64]{3,0,2,1:T(2,128)(2,1)} %copy.56), kind=kOutput, calls=%fused_computation.39 | convolution fusion | flops 2162695 | bytes 1449984 | tf_op jit(solution)/shard_map/div | solution.py:443
  97.5 5.7 %convolution_bitcast_fusion.1 = f32[8,128,8,64]{3,0,2,1:T(8,128)} fusion(bf16[2,128,8,64]{3,0,2,1:T(2,128)(2,1)} %copy.56, f32[2,8,128,8]{1,0,3,2:T(2,128)} %get-tuple-element.85, f32[2,8,128,8]{1,0,3,2:T(2,128)} %convolution_bitcast_fusion.6, f32[2,128,8]{0,2,1:T(8,128)} %get-tuple-element.84), kind=kOutput, calls=%fused_computation.1 | convolution fusion | flops 2146304 | bytes 2498560 | tf_op jit(solution)/shard_map/abth,athe->bthe/dot_general | solution.py:459
  103.1 4.8 %copy.67 = f32[8,128,8,64]{1,3,2,0:T(8,128)} copy(f32[8,128,8,64]{3,0,2,1:T(8,128)} %convolution_bitcast_fusion.1) | data formatting | bytes 4194304 | tf_op jit(solution)/shard_map/abth,athe->bthe/transpose | solution.py:459
  109.3 2.9 %convolution_bitcast_fusion = f32[8,128,8,64]{3,0,2,1:T(8,128)} fusion(bf16[2,128,8,64]{3,0,2,1:T(2,128)(2,1)S(1)} %copy-done.14, f32[2,8,128,8]{1,0,3,2:T(2,128)S(1)} %copy-done.15), kind=kOutput, calls=%fused_computation | convolution fusion | flops 2097152 | bytes 2424832 | tf_op jit(solution)/shard_map/abth,athe->bthe/dot_general | solution.py:460
  112.2 4.8 %copy.70 = f32[8,128,8,64]{1,3,2,0:T(8,128)} copy(f32[8,128,8,64]{3,0,2,1:T(8,128)} %convolution_bitcast_fusion) | data formatting | bytes 4194304 | tf_op jit(solution)/shard_map/abth,athe->bthe/transpose | solution.py:460
  118.6 3.2 %fusion.2 = bf16[2,128,8,64]{3,0,2,1:T(2,128)(2,1)} fusion(bf16[8,128,8,64]{3,0,2,1:T(8,128)(2,1)S(1)} %copy-done.7, f32[2,8,128,8]{1,0,3,2:T(2,128)} %get-tuple-element.85), kind=kOutput, calls=%fused_computation.26 | convolution fusion | flops 2097152 | bytes 1376256 | tf_op jit(solution)/shard_map/abth,bthe->athe/dot_general | solution.py:444
  121.8 1.9 copy.58
  123.8 3.9 %fusion.3 = bf16[2,128,8,64]{3,0,2,1:T(2,128)(2,1)S(1)} fusion(bf16[8,128,8,64]{3,0,2,1:T(8,128)(2,1)} %copy.55, f32[2,8,128,8]{1,0,3,2:T(2,128)} %get-tuple-element.85, f32[2,8,128,8]{1,0,3,2:T(2,128)} %convolution_bitcast_fusion.6, f32[2,128,8]{0,2,1:T(8,128)} %get-tuple-element.84), kind=kOutput, calls=%fused_computation.27 | convolution fusion | flops 2277376 | bytes 1449984 | tf_op jit(solution)/shard_map/abth,bthe->athe/dot_general | solution.py:458
  132.4 7.3 %reduce-scatter.3.cloned.1.call-done = f32[2,128,512]{1,2,0:T(8,128)} async-done(((f32[8,128,512]{1,2,0:T(8,128)}), f32[2,128,512]{1,2,0:T(8,128)}) %reduce-scatter.3.cloned.1.call-update) | async-done | bytes 524304 | tf_op jit(solution)/shard_map/reduce_scatter | solution.py:501
  139.7 2.5 convolution_add_fusion.1
  142.2 31.8 %reduce-scatter.5.cloned.1.call-done = f32[2,128,512]{1,2,0:T(8,128)} async-done(((f32[8,128,512]{1,2,0:T(8,128)}), f32[2,128,512]{1,2,0:T(8,128)}) %reduce-scatter.5.cloned.1.call-update) | async-done | bytes 524304 | tf_op jit(solution)/shard_map/reduce_scatter | solution.py:502
  174.1 3.5 %fusion.66 = (f32[512]{0:T(512)}, f32[512]{0:T(512)}, f32[512]{0:T(512)}, f32[512]{0:T(512)}, f32[512]{0:T(512)}, /*index=5*/f32[512]{0:T(512)}, f32[512]{0:T(51...) fusion(bf16[2,143,512]{2,1,0:T(8,128)(2,1)S(1)} %constant_dynam, ...), kind=kOutput, calls=%fused_computation.161 | convolution fusion | flops 141550080 | bytes 6846464 | tf_op jit(solution)/shard_map/dot_general | solution.py:466
  178.9 4.2 %collective-permute-start.2 = (bf16[2,15,512]{2,1,0:T(8,128)(2,1)S(1)}, bf16[2,15,512]{2,1,0:T(8,128)(2,1)S(1)}, u32[]{:S(2)}, u32[]{:S(2)}) collective-permute-start(bf16[2,15,512]{2,1,0:T(8,128)(2,1)S(1)} %get-tuple-element.49), channel_id=1, source_target_pairs={{0,1},{1,2},{2,3},{3,4},{4,5},{5,6},{6,7},{7,8},{8,9},{9,10},{10,1... | collective-permute-start | bytes 92168 | tf_op jit(solution)/shard_map/ppermute | solution.py:394
  188.7 50.3 %shard_map.126 = (bf16[4,512,512]{2,1,0:T(8,128)(2,1)S(1)}, f32[32,512]{1,0:T(8,128)S(1)}) custom-call(f32[512,512]{1,0:T(8,128)S(1)} %convolution_bitcast_fusion.5.q_ref, f32[512,512]{1,0:T(8,128)S(1)} %convolution_bitcast_fusion.4.k_ref, f32[512,512]{1,0:T(8,128)S(1)} %convolution_bitcast_fusion.3.v_ref, f32[512,512]{1,0:T(8,128)S(1)} %convolution_bitcast_fusion.2.o_ref, ...), custom_call_target="tpu_custom_call" | custom-call | tf_op jit(solution)/shard_map/pallas_call | solution.py:344
  239.2 2.2 bitcast_convert_fusion
  241.7 2.8 %fusion.70 = bf16[2,128,512]{2,1,0:T(8,128)(2,1)} fusion(f32[2,158,512]{2,1,0:T(8,128)S(1)} %maximum_convert_fusion, bf16[2,128,512]{2,1,0:T(8,128)(2,1)S(1)} %copy-done.3, f32[512]{0:T(512)S(1)} %bitcast.181, f32[512]{0:T(512)S(1)} %bitcast.183, f32[512]{0:T(512)S(1)} %bitcast.187, f32[512]{0:T(512)S(1)} %bitcast.189, f32[512]{0:T(512)S(1)} %bitcast.191, ...), kind=kLoop, calls=%fused_computation.166 | loop fusion | flops 8388608 | bytes 16840704 | tf_op jit(solution)/shard_map/convert_element_type | solution.py:516
  (122 shorter events, 27.8 us)
Async XLA Ops:
  7.2 16.8 %copy-start = (bf16[512,512]{1,0:T(8,128)(2,1)S(1)}, bf16[512,512]{1,0:T(8,128)(2,1)}, u32[]{:S(2)}) copy-start(bf16[512,512]{1,0:T(8,128)(2,1)} %param.12) | copy-start | bytes 1572868
  7.2 49.1 %all-gather.3.cloned.1.call-start = ((), (), s32[]{:S(2)}) async-start(), calls=%async_computation.2 | async-start | bytes 1310720 | tf_op jit(solution)/shard_map/all_gather | solution.py:492
  8.1 9.2 %collective-permute-start.1 = (bf16[2,15,512]{2,1,0:T(8,128)(2,1)S(1)}, bf16[2,15,512]{2,1,0:T(8,128)(2,1)S(1)}, u32[]{:S(2)}, u32[]{:S(2)}) collective-permute-start(bf16[2,15,512]{2,1,0:T(8,128)(2,1)S(1)} %get-tuple-element.52), channel_id=1, source_target_pairs={{1,0},{2,1},{3,2},{4,3},{5,4},{6,5},{7,6},{8,7},{9,8},{10,9},{11,1... | collective-permute-start | bytes 92168 | tf_op jit(solution)/shard_map/ppermute | solution.py:395
  9.4 7.9 %collective-permute-start = (bf16[2,15,512]{2,1,0:T(8,128)(2,1)S(1)}, bf16[2,15,512]{2,1,0:T(8,128)(2,1)S(1)}, u32[]{:S(2)}, u32[]{:S(2)}) collective-permute-start(bf16[2,15,512]{2,1,0:T(8,128)(2,1)S(1)} %get-tuple-element.51), channel_id=1, source_target_pairs={{0,1},{1,2},{2,3},{3,4},{4,5},{5,6},{6,7},{7,8},{8,9},{9,10},{10,1... | collective-permute-start | bytes 92168 | tf_op jit(solution)/shard_map/ppermute | solution.py:394
  16.1 7.7 %copy-start.18 = (f32[1,512]{1,0:T(1,128)}, f32[1,512]{1,0:T(1,128)S(1)}, u32[]{:S(2)}) copy-start(f32[1,512]{1,0:T(1,128)S(1)} %get-tuple-element.61) | copy-start | bytes 6148
  16.2 7.7 %copy-start.20 = (f32[1,512]{1,0:T(1,128)}, f32[1,512]{1,0:T(1,128)S(1)}, u32[]{:S(2)}) copy-start(f32[1,512]{1,0:T(1,128)S(1)} %get-tuple-element.62) | copy-start | bytes 6148
  16.2 7.7 %copy-start.22 = (f32[1,512]{1,0:T(1,128)}, f32[1,512]{1,0:T(1,128)S(1)}, u32[]{:S(2)}) copy-start(f32[1,512]{1,0:T(1,128)S(1)} %get-tuple-element.63) | copy-start | bytes 6148
  16.2 7.7 %copy-start.24 = (f32[1,512]{1,0:T(1,128)}, f32[1,512]{1,0:T(1,128)S(1)}, u32[]{:S(2)}) copy-start(f32[1,512]{1,0:T(1,128)S(1)} %get-tuple-element.64) | copy-start | bytes 6148
  16.2 7.7 %copy-start.26 = (f32[1,512]{1,0:T(1,128)}, f32[1,512]{1,0:T(1,128)S(1)}, u32[]{:S(2)}) copy-start(f32[1,512]{1,0:T(1,128)S(1)} %get-tuple-element.65) | copy-start | bytes 6148
  16.2 7.7 %copy-start.28 = (f32[1,512]{1,0:T(1,128)}, f32[1,512]{1,0:T(1,128)S(1)}, u32[]{:S(2)}) copy-start(f32[1,512]{1,0:T(1,128)S(1)} %get-tuple-element.66) | copy-start | bytes 6148
  16.2 7.7 %copy-start.30 = (f32[1,512]{1,0:T(1,128)}, f32[1,512]{1,0:T(1,128)S(1)}, u32[]{:S(2)}) copy-start(f32[1,512]{1,0:T(1,128)S(1)} %get-tuple-element.67) | copy-start | bytes 6148
  16.2 7.7 %copy-start.32 = (f32[1,512]{1,0:T(1,128)}, f32[1,512]{1,0:T(1,128)S(1)}, u32[]{:S(2)}) copy-start(f32[1,512]{1,0:T(1,128)S(1)} %get-tuple-element.68) | copy-start | bytes 6148
  16.2 7.7 %copy-start.34 = (f32[1,512]{1,0:T(1,128)}, f32[1,512]{1,0:T(1,128)S(1)}, u32[]{:S(2)}) copy-start(f32[1,512]{1,0:T(1,128)S(1)} %get-tuple-element.69) | copy-start | bytes 6148
  16.2 7.7 %copy-start.36 = (f32[1,512]{1,0:T(1,128)}, f32[1,512]{1,0:T(1,128)S(1)}, u32[]{:S(2)}) copy-start(f32[1,512]{1,0:T(1,128)S(1)} %get-tuple-element.70) | copy-start | bytes 6148
  16.2 7.7 %copy-start.38 = (f32[1,512]{1,0:T(1,128)}, f32[1,512]{1,0:T(1,128)S(1)}, u32[]{:S(2)}) copy-start(f32[1,512]{1,0:T(1,128)S(1)} %get-tuple-element.71) | copy-start | bytes 6148
  17.3 7.8 %copy-start.13 = (bf16[512,512]{1,0:T(8,128)(2,1)S(1)}, bf16[512,512]{1,0:T(8,128)(2,1)}, u32[]{:S(2)}) copy-start(bf16[512,512]{1,0:T(8,128)(2,1)} %param.11) | copy-start | bytes 1572868
  25.0 57.9 %all-gather.5.cloned.1.call-start = ((), (), s32[]{:S(2)}) async-start(), calls=%async_computation.3 | async-start | bytes 1310720 | tf_op jit(solution)/shard_map/all_gather | solution.py:491
  26.1 113.6 %reduce-scatter.3.cloned.1.call-start = ((), (), s32[]{:S(2)}) async-start(), calls=%async_computation.4 | async-start | bytes 2621440 | tf_op jit(solution)/shard_map/reduce_scatter | solution.py:501
  88.3 4.0 %copy-start.8 = (bf16[8,128,8,64]{3,0,2,1:T(8,128)(2,1)S(1)}, bf16[8,128,8,64]{3,0,2,1:T(8,128)(2,1)}, u32[]{:S(2)}) copy-start(bf16[8,128,8,64]{3,0,2,1:T(8,128)(2,1)} %copy.55) | copy-start | bytes 3145732
  107.9 66.1 %reduce-scatter.5.cloned.1.call-start = ((), (), s32[]{:S(2)}) async-start(), calls=%async_computation.5 | async-start | bytes 2621440 | tf_op jit(solution)/shard_map/reduce_scatter | solution.py:502
  128.2 3.1 %copy-start.12 = (bf16[512,512]{1,0:T(8,128)(2,1)S(1)}, bf16[512,512]{1,0:T(8,128)(2,1)}, u32[]{:S(2)}) copy-start(bf16[512,512]{1,0:T(8,128)(2,1)} %param.10) | copy-start | bytes 1572868
  177.6 6.7 %copy-start.16 = (bf16[2,128,512]{2,1,0:T(8,128)(2,1)}, bf16[2,128,512]{2,1,0:T(8,128)(2,1)S(1)}, u32[]{:S(2)}) copy-start(bf16[2,128,512]{2,1,0:T(8,128)(2,1)S(1)} %get-tuple-element.48) | copy-start | bytes 786436
  177.6 63.8 %collective-permute-start.3 = (bf16[2,15,512]{2,1,0:T(8,128)(2,1)S(1)}, bf16[2,15,512]{2,1,0:T(8,128)(2,1)S(1)}, u32[]{:S(2)}, u32[]{:S(2)}) collective-permute-start(bf16[2,15,512]{2,1,0:T(8,128)(2,1)S(1)} %get-tuple-element.50), channel_id=1, source_target_pairs={{1,0},{2,1},{3,2},{4,3},{5,4},{6,5},{7,6},{8,7},{9,8},{10,9},{11,1... | collective-permute-start | bytes 92168 | tf_op jit(solution)/shard_map/ppermute | solution.py:395
  178.9 62.5 %collective-permute-start.2 = (bf16[2,15,512]{2,1,0:T(8,128)(2,1)S(1)}, bf16[2,15,512]{2,1,0:T(8,128)(2,1)S(1)}, u32[]{:S(2)}, u32[]{:S(2)}) collective-permute-start(bf16[2,15,512]{2,1,0:T(8,128)(2,1)S(1)} %get-tuple-element.49), channel_id=1, source_target_pairs={{0,1},{1,2},{2,3},{3,4},{4,5},{5,6},{6,7},{7,8},{8,9},{9,10},{10,1... | collective-permute-start | bytes 92168 | tf_op jit(solution)/shard_map/ppermute | solution.py:394
  (24 other events, 53.7 us)
Sparse Core Ops, SparseCore 0:
  25.2 31.0 all-gather.2
  58.7 24.2 all-gather.4
  108.1 31.6 reduce-scatter.2
  142.3 31.7 reduce-scatter.4

commit v2 on v0

v2 whole, which is shorter than its diff:
```python
import math
import types

import jax
import jax.numpy as jnp
from jax import lax
from jax.experimental import pallas as pl
from jax.experimental.pallas import tpu as pltpu
from jax.sharding import PartitionSpec as P

HEADS = 8
FRAMES = 128
SHARE = 32
NX, NY, NZ = 4, 4, 8
MESH = pl.DeviceIdType.MESH


class Place:
    def __init__(self):
        mic = lax.axis_index("mic")
        tm = lax.axis_index("tm")
        self.mic, self.tm = mic, tm
        self.core = lax.rem(mic, 2)
        self.x = lax.rem(tm, NX)
        self.z = lax.rem(lax.div(tm, NX), NZ)
        self.y = lax.div(tm, NX * NZ) * 2 + lax.div(mic, 2)

    def device(self, x=None, y=None, z=None, core=None):
        x = self.x if x is None else x
        y = self.y if y is None else y
        z = self.z if z is None else z
        core = self.core if core is None else core
        mic = lax.rem(y, 2) * 2 + core
        tm = lax.div(y, 2) * (NX * NZ) + z * NX + x
        return (mic, tm)

    def along(self, axis, step):
        size = {"x": NX, "y": NY, "z": NZ, "core": 2}[axis]
        index = lax.rem(getattr(self, axis) + step, size)
        return index, self.device(**{axis: index})


def rows_at(start, count):
    return pl.ds(pl.multiple_of(start, count), count)


def send(src, dst, send_sem, recv_sem, device):
    copy = pltpu.make_async_remote_copy(
        src_ref=src,
        dst_ref=dst,
        send_sem=send_sem,
        recv_sem=recv_sem,
        device_id=device,
        device_id_type=MESH,
    )
    copy.start()
    return copy


def greet(peers):
    barrier = pltpu.get_barrier_semaphore()
    for peer in peers:
        pl.semaphore_signal(barrier, inc=1, device_id=peer, device_id_type=MESH)
    pl.semaphore_wait(barrier, len(peers))


SIZES = {"x": NX, "y": NY, "z": NZ, "core": 2}
HALF, STREAM, FIRST, SECOND, TILE = 4096, 2048, 512, 128, 16
ORDERS = (("x", "y", "z"), ("y", "x", "z"))


def f32(value):
    return value.astype(jnp.float32)


def dot(left, right, left_dim=1, right_dim=0):
    return lax.dot_general(
        left, right, (((left_dim,), (right_dim,)), ((), ())), preferred_element_type=jnp.float32
    )


def lanes(block):
    return pl.ds(pl.multiple_of(block * 128, 128), 128)


def shifted(padded):
    for low in range(8):
        rolled = padded if low == 0 else pltpu.roll(padded, padded.shape[0] - low, 0)
        for high in range(4):
            if high * 8 + low:
                yield high * 8 + low, rolled[high * 8 : high * 8 + FRAMES, :]


def kernel_body(
    scale,
    frames,
    cotangent,
    taps,
    w_query,
    w_key,
    w_value,
    w_out,
    layer_out,
    frame_grad,
    tap_out,
    grads_out,
    m,
):
    bf16 = jnp.bfloat16
    here = Place()
    group = [lax.rem(here.mic + step, 4) for step in range(1, 4)]
    after = (here.mic, lax.rem(here.tm + 1, NX * NY * NZ // 2))
    before = (here.mic, lax.rem(here.tm + NX * NY * NZ // 2 - 1, NX * NY * NZ // 2))
    peers = [after, before]
    peers += [(mic, here.tm) for mic in group]
    for axis in ("core", "x", "y", "z"):
        for step in range(1, SIZES[axis]):
            peers.append(here.along(axis, step)[1])
    greet(peers)
    sent = []

    halo = [
        send(frames.at[:, pl.ds(FRAMES - 16, 16), :], m.halo.at[0], m.hs.at[0], m.hr.at[0], after),
        send(frames.at[:, pl.ds(0, 16), :], m.halo.at[1], m.hs.at[1], m.hr.at[1], before),
    ]
    mics_here = pl.ds(here.mic * 2, 2)
    share_here = rows_at(here.mic * SHARE, SHARE)
    cot_copies = []
    for step, mic in enumerate(group):
        cot_copies.append(
            send(
                cotangent.at[:, rows_at(mic * SHARE, SHARE), :],
                m.cot_all.at[mics_here],
                m.cs.at[step],
                m.cr.at[step],
                (mic, here.tm),
            )
        )
    sent += halo + cot_copies
    m.cot_all[mics_here] = cotangent[:, share_here, :]
    for block in range(4):
        m.taps4[block, 0:31] = taps[:, block * 128 : (block + 1) * 128]
        for mic in range(2):
            m.fpad[mic, block, 16 : 16 + FRAMES] = f32(
                frames[mic, :, block * 128 : (block + 1) * 128]
            )
    row = lax.broadcasted_iota(jnp.int32, (512, 128), 0)
    col = lax.broadcasted_iota(jnp.int32, (512, 128), 1)
    m.gather_heads[...] = jnp.where(lax.div(row, 64) == col, 1.0, 0.0).astype(bf16)
    row = lax.broadcasted_iota(jnp.int32, (128, 512), 0)
    col = lax.broadcasted_iota(jnp.int32, (128, 512), 1)
    m.spread_heads[...] = jnp.where(lax.div(col, 64) == row, 1.0, 0.0).astype(bf16)

    def fill_halo(side, pad, buffer, copy):
        copy.wait_recv()
        inside = here.tm > 0 if side == 0 else here.tm < NX * NY * NZ // 2 - 1
        rows = slice(0, 16) if side == 0 else slice(16 + FRAMES, 32 + FRAMES)
        for mic in range(2):
            for block in range(4):
                value = f32(buffer[side, mic, :, block * 128 : (block + 1) * 128])
                pad[mic, block, rows] = jnp.where(inside, value, 0.0)

    for side in range(2):
        fill_halo(side, m.fpad, m.halo, halo[side])

    act_copies = []
    for mic in range(2):

        def conv_block(block, carry):
            padded = m.fpad[mic, block]
            conv = jnp.zeros((FRAMES, 128), jnp.float32)
            for offset, rows in shifted(padded):
                conv = conv + rows * m.taps4[block, offset - 1 : offset]
            sig = 1.0 / (1.0 + jnp.exp(-conv))
            m.acted[mic, :, lanes(block)] = (conv * sig).astype(bf16)
            m.dsilu[mic, block] = sig * (1.0 + conv * (1.0 - sig))
            return carry

        lax.fori_loop(0, 4, conv_block, 0)
        for step, target in enumerate(group):
            act_copies.append(
                send(
                    m.acted.at[mic, rows_at(target * SHARE, SHARE), :],
                    m.act_all.at[here.mic * 2 + mic],
                    m.acs.at[mic, step],
                    m.acr.at[mic, step],
                    (target, here.tm),
                )
            )
        m.act_all[here.mic * 2 + mic] = m.acted[mic, share_here, :]
    sent += act_copies

    width = frames.shape[2]
    rows = 8 * SHARE
    for copy in cot_copies:
        copy.wait_recv()
    cot_rows = m.cot_all[...].reshape(rows, width)
    m.ups[...] = dot(cot_rows, w_out[...], 1, 1).astype(bf16).reshape(8, SHARE, width)
    for copy in act_copies:
        copy.wait_recv()
    act_rows = m.act_all[...].reshape(rows, width)
    for weight, target in ((w_query, m.queries), (w_key, m.keys), (w_value, m.values)):
        target[...] = dot(act_rows, weight[...]).astype(bf16).reshape(8, SHARE, width)

    m.dkey[...] = jnp.zeros_like(m.dkey)
    m.dvalue[...] = jnp.zeros_like(m.dvalue)
    factor = 1.0 / math.sqrt(width // HEADS)

    def attend(index, carry):
        query, up = m.queries[index], m.ups[index]
        keys, values = m.keys[...], m.values[...]
        gather, spread = m.gather_heads[...], m.spread_heads[...]

        def per_head(product):
            return dot(product.reshape(rows, width), gather).reshape(8, SHARE, 128)

        def per_lane(heads):
            return dot(heads.astype(bf16).reshape(rows, 128), spread).reshape(8, SHARE, width)

        weights = jnp.exp(per_head(query[None] * keys) * factor)
        weights = weights / jnp.sum(weights, axis=0, keepdims=True)
        products = per_head(up[None] * values)
        inner = weights * (products - jnp.sum(weights * products, axis=0, keepdims=True)) * factor
        weights, inner = per_lane(weights), per_lane(inner)
        m.mixed[index] = jnp.sum(weights * f32(values), axis=0).astype(bf16)
        m.dquery[index] = jnp.sum(inner * f32(keys), axis=0).astype(bf16)
        m.dkey[...] += inner * f32(query)[None]
        m.dvalue[...] += weights * f32(up)[None]
        return carry

    lax.fori_loop(0, 8, attend, 0)

    mixed = m.mixed[...].reshape(rows, width)
    dquery = m.dquery[...].reshape(rows, width)
    dkey = m.dkey[...].astype(bf16).reshape(rows, width)
    dvalue = m.dvalue[...].astype(bf16).reshape(rows, width)
    dacted = dot(dquery, w_query[...], 1, 1)
    dacted = dacted + dot(dkey, w_key[...], 1, 1)
    dacted = dacted + dot(dvalue, w_value[...], 1, 1)
    m.dacted[...] = dacted.astype(bf16).reshape(8, SHARE, width)
    home_copies = []
    for kind, (source, target) in enumerate(((m.dacted, m.dacted_home), (m.mixed, m.mixed_home))):
        copies = []
        for step, mic in enumerate(group):
            copies.append(
                send(
                    source.at[pl.ds(mic * 2, 2)],
                    target.at[:, share_here, :],
                    m.bs.at[kind, step],
                    m.br.at[kind, step],
                    (mic, here.tm),
                )
            )
        target[:, share_here, :] = source[mics_here]
        home_copies.append(copies)
        sent += copies

    act_turned = act_rows.T
    for g, (left, right) in enumerate(
        ((act_turned, dquery), (act_turned, dkey), (act_turned, dvalue), (mixed.T, cot_rows))
    ):
        term = dot(left, right).astype(bf16)
        for block in range(4):
            at = (g * 4 + block) * 512
            m.mine[at : at + 512, :] = term[:, block * 128 : (block + 1) * 128]

    own = here.core * HALF
    other, sibling = here.along("core", 1)
    core_copies = []
    for s in range(2):
        core_copies.append(
            send(
                m.mine.at[rows_at(other * HALF + s * STREAM, STREAM)],
                m.core_rx.at[s],
                m.core_s.at[s],
                m.core_r.at[s],
                sibling,
            )
        )
    sent += core_copies

    for copy in home_copies[0]:
        copy.wait_recv()

    def dconv_block(step, carry):
        mic, block = lax.div(step, 4), lax.rem(step, 4)
        dconv = f32(m.dacted_home[mic, :, lanes(block)]) * m.dsilu[mic, block]
        m.gpad[mic, block, 16 : 16 + FRAMES] = dconv
        m.ends[0, mic, :, lanes(block)] = dconv[FRAMES - 16 :].astype(bf16)
        m.ends[1, mic, :, lanes(block)] = dconv[:16].astype(bf16)
        return carry

    lax.fori_loop(0, 8, dconv_block, 0)
    ghalo = [
        send(m.ends.at[0], m.ghalo.at[0], m.hs.at[2], m.hr.at[2], after),
        send(m.ends.at[1], m.ghalo.at[1], m.hs.at[3], m.hr.at[3], before),
    ]
    sent += ghalo

    first = []
    for s in range(2):
        core_copies[s].wait_recv()
        part = rows_at(own + s * STREAM, STREAM)
        m.mine[part, :] = (f32(m.mine[part, :]) + f32(m.core_rx[s])).astype(bf16)
        axis = ORDERS[s][0]
        copies = []
        for step in range(1, SIZES[axis]):
            index, peer = here.along(axis, step)
            copies.append(
                send(
                    m.mine.at[rows_at(own + s * STREAM + index * FIRST, FIRST)],
                    m.rx1.at[s, step - 1],
                    m.s1.at[s, step - 1],
                    m.r1.at[s, step - 1],
                    peer,
                )
            )
        first.append(copies)
        sent += copies

    def tap_block(block, carry):
        sums = {}
        for mic in range(2):
            dconv = m.gpad[mic, block, 16 : 16 + FRAMES]
            for offset, rows_in in shifted(m.fpad[mic, block]):
                part = jnp.sum((rows_in * dconv).reshape(FRAMES // 8, 8, 128), axis=0)
                sums[offset] = sums[offset] + part if mic else part
        for offset, part in sums.items():
            m.tap0[block, offset - 1 : offset] = jnp.sum(part, axis=0, keepdims=True)
        m.tap0[block, 31:32] = jnp.zeros((1, 128), jnp.float32)
        return carry

    lax.fori_loop(0, 4, tap_block, 0)

    def tap_tile(index):
        return lax.div(index, 2), rows_at(lax.rem(index, 2) * 16, 16)

    tap_copies = []
    for step in range(1, NZ):
        index, peer = here.along("z", step)
        block, part = tap_tile(index)
        tap_copies.append(
            send(
                m.tap0.at[block, part],
                m.tap_zrx.at[step - 1],
                m.ts.at[step - 1],
                m.tr.at[step - 1],
                peer,
            )
        )
    sent += tap_copies

    for copy in home_copies[1]:
        copy.wait_recv()
    home_rows = m.mixed_home[...].reshape(2 * FRAMES, width)
    layer_out[...] = (
        f32(frames[...]) + dot(home_rows, w_out[...]).reshape(2, FRAMES, width)
    ).astype(bf16)

    second = []
    for s in range(2):
        axis, axis2, _ = ORDERS[s]
        place = own + s * STREAM + getattr(here, axis) * FIRST
        for copy in first[s]:
            copy.wait_recv()
        part = rows_at(place, FIRST)
        total = f32(m.mine[part, :])
        for step in range(SIZES[axis] - 1):
            total = total + f32(m.rx1[s, step])
        m.mine[part, :] = total.astype(bf16)
        copies = []
        for step in range(1, SIZES[axis2]):
            index, peer = here.along(axis2, step)
            copies.append(
                send(
                    m.mine.at[rows_at(place + index * SECOND, SECOND)],
                    m.rx2.at[s, step - 1],
                    m.s2.at[s, step - 1],
                    m.r2.at[s, step - 1],
                    peer,
                )
            )
        second.append((place, copies))
        sent += copies

    block, part = tap_tile(here.z)
    total = m.tap0[block, part]
    for step in range(1, NZ):
        tap_copies[step - 1].wait_recv()
        total = total + m.tap_zrx[step - 1]

    def tap_axis(tile, axis, base):
        slot = base + getattr(here, axis)
        m.tap_rx[slot] = tile
        copies = []
        for step in range(1, SIZES[axis]):
            copies.append(
                send(
                    m.tap_rx.at[slot],
                    m.tap_rx.at[slot],
                    m.ts.at[NZ - 1 + base + step - 1],
                    m.tr.at[NZ - 1 + base + step - 1],
                    here.along(axis, step)[1],
                )
            )
        return copies

    def tap_sum(copies, base):
        for copy in copies:
            copy.wait_recv()
        total = m.tap_rx[base]
        for index in range(len(copies)):
            total = total + m.tap_rx[base + 1 + index]
        return total

    tap_x = tap_axis(total, "x", 0)
    sent += tap_x

    for side in range(2):
        fill_halo(side, m.gpad, m.ghalo, ghalo[side])

    def grad_block(step, carry):
        mic, block = lax.div(step, 4), lax.rem(step, 4)
        total = f32(cotangent[mic, :, lanes(block)])
        for offset, rows_in in shifted(m.gpad[mic, block]):
            total = total + rows_in * m.taps4[block, 31 - offset : 32 - offset]
        frame_grad[mic, :, lanes(block)] = total.astype(bf16)
        return carry

    lax.fori_loop(0, 8, grad_block, 0)

    third = []
    for s in range(2):
        axis2 = ORDERS[s][1]
        place, copies = second[s]
        place = place + getattr(here, axis2) * SECOND
        for copy in copies:
            copy.wait_recv()
        part = rows_at(place, SECOND)
        total = f32(m.mine[part, :])
        for step in range(SIZES[axis2] - 1):
            total = total + f32(m.rx2[s, step])
        m.mine[part, :] = total.astype(bf16)
        copies = []
        for step in range(1, NZ):
            index, peer = here.along("z", step)
            copies.append(
                send(
                    m.mine.at[rows_at(place + index * TILE, TILE)],
                    m.rx3.at[s, step - 1],
                    m.s3.at[s, step - 1],
                    m.r3.at[s, step - 1],
                    peer,
                )
            )
        third.append((place, copies))
        sent += copies

    tap_y = tap_axis(tap_sum(tap_x, 0), "y", 4)
    sent += tap_y

    def gather(s, level, axis, place, count):
        copies = []
        base = (0, NZ - 1, NZ + 2)[level]
        part = rows_at(place, count)
        for step in range(1, SIZES[axis]):
            copies.append(
                send(
                    m.full.at[part],
                    m.full.at[part],
                    m.gs.at[s, base + step - 1],
                    m.gr.at[s, base + step - 1],
                    here.along(axis, step)[1],
                )
            )
        return copies

    back = []
    for s in range(2):
        place, copies = third[s]
        for copy in copies:
            copy.wait_recv()
        part = rows_at(place + here.z * TILE, TILE)
        total = f32(m.mine[part, :])
        for step in range(NZ - 1):
            total = total + f32(m.rx3[s, step])
        m.full[part, :] = (total * scale).astype(bf16)
        copies = gather(s, 0, "z", place + here.z * TILE, TILE)
        back.append((place, copies))
        sent += copies

    tap_c = tap_axis(tap_sum(tap_y, 4), "core", 8)
    sent += tap_c

    for level in (1, 2):
        for s in range(2):
            place, copies = back[s]
            for copy in copies:
                copy.wait_recv()
            axis = ORDERS[s][2 - level]
            count = (TILE, SECOND, FIRST)[level]
            copies = gather(s, level, axis, place, count)
            back[s] = (place - getattr(here, axis) * count, copies)
            sent += copies
        if level == 1:
            block, part = tap_tile(here.z)
            m.tap_full[block, part] = tap_sum(tap_c, 8) * scale
            tap_back = []
            for step in range(1, NZ):
                tap_back.append(
                    send(
                        m.tap_full.at[block, part],
                        m.tap_full.at[block, part],
                        m.tgs.at[step - 1],
                        m.tgr.at[step - 1],
                        here.along("z", step)[1],
                    )
                )
            sent += tap_back
    last = []
    for s in range(2):
        place, copies = back[s]
        for copy in copies:
            copy.wait_recv()
        part = rows_at(own + s * STREAM, STREAM)
        copy = send(m.full.at[part], m.full.at[part], m.gcs.at[s], m.gcr.at[s], sibling)
        last.append(copy)
    sent += last
    for copy in tap_back:
        copy.wait_recv()
    for block in range(4):
        tap_out[:, block * 128 : (block + 1) * 128] = m.tap_full[block, 0:31]
    for copy in last:
        copy.wait_recv()
    for g in range(4):
        for block in range(4):
            at = (g * 4 + block) * 512
            grads_out[g, :, block * 128 : (block + 1) * 128] = m.full[at : at + 512, :]
    for copy in sent:
        copy.wait_send()


def memory(width):
    bf16, full = jnp.bfloat16, jnp.float32
    dma = pltpu.SemaphoreType.DMA
    rows = (8, SHARE, width)
    home = (2, FRAMES, width)
    wide = (2, 4, FRAMES + 32, 128)
    return dict(
        halo=pltpu.VMEM((2, 2, 16, width), bf16),
        ghalo=pltpu.VMEM((2, 2, 16, width), bf16),
        ends=pltpu.VMEM((2, 2, 16, width), bf16),
        cot_all=pltpu.VMEM(rows, bf16),
        act_all=pltpu.VMEM(rows, bf16),
        acted=pltpu.VMEM(home, bf16),
        taps4=pltpu.VMEM((4, 32, 128), full),
        fpad=pltpu.VMEM(wide, full),
        gpad=pltpu.VMEM(wide, full),
        dsilu=pltpu.VMEM((2, 4, FRAMES, 128), full),
        gather_heads=pltpu.VMEM((width, 128), bf16),
        spread_heads=pltpu.VMEM((128, width), bf16),
        queries=pltpu.VMEM(rows, bf16),
        keys=pltpu.VMEM(rows, bf16),
        values=pltpu.VMEM(rows, bf16),
        ups=pltpu.VMEM(rows, bf16),
        mixed=pltpu.VMEM(rows, bf16),
        dquery=pltpu.VMEM(rows, bf16),
        dkey=pltpu.VMEM(rows, full),
        dvalue=pltpu.VMEM(rows, full),
        dacted=pltpu.VMEM(rows, bf16),
        dacted_home=pltpu.VMEM(home, bf16),
        mixed_home=pltpu.VMEM(home, bf16),
        mine=pltpu.VMEM((2 * HALF, 128), bf16),
        full=pltpu.VMEM((2 * HALF, 128), bf16),
        core_rx=pltpu.VMEM((2, STREAM, 128), bf16),
        rx1=pltpu.VMEM((2, 3, FIRST, 128), bf16),
        rx2=pltpu.VMEM((2, 3, SECOND, 128), bf16),
        rx3=pltpu.VMEM((2, NZ - 1, TILE, 128), bf16),
        tap0=pltpu.VMEM((4, 32, 128), full),
        tap_zrx=pltpu.VMEM((NZ - 1, 16, 128), full),
        tap_rx=pltpu.VMEM((10, 16, 128), full),
        tap_full=pltpu.VMEM((4, 32, 128), full),
        hs=dma((4,)),
        hr=dma((4,)),
        cs=dma((3,)),
        cr=dma((3,)),
        acs=dma((2, 3)),
        acr=dma((2, 3)),
        bs=dma((2, 3)),
        br=dma((2, 3)),
        core_s=dma((2,)),
        core_r=dma((2,)),
        s1=dma((2, 3)),
        r1=dma((2, 3)),
        s2=dma((2, 3)),
        r2=dma((2, 3)),
        s3=dma((2, NZ - 1)),
        r3=dma((2, NZ - 1)),
        gs=dma((2, NZ + 5)),
        gr=dma((2, NZ + 5)),
        gcs=dma((2,)),
        gcr=dma((2,)),
        ts=dma((NZ + 8,)),
        tr=dma((NZ + 8,)),
        tgs=dma((NZ - 1,)),
        tgr=dma((NZ - 1,)),
    )


def shards(frames, cotangent, kernel, w_query, w_key, w_value, w_out):
    count, length, width = frames.shape
    scale = 1.0 / math.sqrt(lax.axis_size("mic") * count * lax.axis_size("tm") * length)
    scratch = memory(width)

    def body(*refs):
        parts = types.SimpleNamespace(**dict(zip(scratch, refs[11:])))
        kernel_body(scale, *refs[:11], parts)

    layer_out, frame_grad, kernel_grad, grads = pl.pallas_call(
        body,
        out_shape=(
            jax.ShapeDtypeStruct(frames.shape, jnp.bfloat16),
            jax.ShapeDtypeStruct(frames.shape, jnp.bfloat16),
            jax.ShapeDtypeStruct(kernel.shape, jnp.float32),
            jax.ShapeDtypeStruct((4, width, width), jnp.bfloat16),
        ),
        in_specs=[pl.BlockSpec(memory_space=pltpu.VMEM)] * 7,
        out_specs=[pl.BlockSpec(memory_space=pltpu.VMEM)] * 4,
        scratch_shapes=list(scratch.values()),
        compiler_params=pltpu.CompilerParams(
            collective_id=0, has_side_effects=True, vmem_limit_bytes=56 * 2**20
        ),
    )(frames, cotangent, kernel, w_query, w_key, w_value, w_out)
    return (layer_out, frame_grad, kernel_grad) + tuple(f32(grads[g]) for g in range(4))


def solution(mesh):
    in_specs = (P("mic", "tm", None), P("mic", "tm", None), P(), P(), P(), P(), P())
    out_specs = (P("mic", "tm", None), P("mic", "tm", None), P(), P(), P(), P(), P())
    return jax.shard_map(shards, mesh=mesh, in_specs=in_specs, out_specs=out_specs, check_vma=False)
```

time: 462 us -> 78.9 us (0.17)
  waiting for transfers between devices: 264 us -> 0 us
  blocking collectives: 83 us -> 0 us
  Pallas kernels: 0 us -> 72.2 us
  matrix products: 38.1 us -> 0 us
  local copies, waits for them, and re-layouts: 33.6 us -> 2.05 us
  between operations: 14.4 us -> 0.67 us
  starting transfers between devices: 11.8 us -> 0 us
  other arithmetic: 15.5 us -> 3.81 us
    psum x1 -> x0, waiting for transfers between devices: 176 us -> none  [shards(): lax.psum((tap_term, query_term, key_term, value_term, out_term), ('mic',...]
    psum x1 -> x0, blocking collectives: 83 us -> none  [shards(): lax.psum((tap_term, query_term, key_term, value_term, out_term), ('mic',...]
    pallas_call x0 -> x1, Pallas kernels: none -> 72.2 us  [shards(): pl.pallas_call(body, out_shape=(jax.ShapeDtypeStruct(frames.shape, jnp.bf...]
    all_gather x2 -> x0, waiting for transfers between devices: 48 us -> none  [the longest x1 26.8 us: shards(): lax.all_gather(value_rows, 'mic', axis=0, tiled=True)]
    reduce_scatter x2 -> x0, waiting for transfers between devices: 40.2 us -> none  [the longest x1 32 us: shards(): lax.psum_scatter(value_terms, 'mic', scatter_dimension=0, tiled=True)]
    dot_general x17 -> x0, matrix products: 33 us -> none  [the longest x4 7.31 us: outer(): jnp.dot(left.reshape(-1, width).T, right.reshape(-1, right.shape[-1]), pr...]
    ppermute x4 -> x0, starting transfers between devices: 11.1 us -> none  [the longest x2 8.56 us: extended(): before = lax.ppermute(last, axis, up)]
    reshape x4 -> x0, local copies, waits for them, and re-layouts: 9.76 us -> none  [split_heads(): rows.astype(jnp.float32)]
  transfers between devices with their start and end apart: 9 -> 0, of which waited for: 5 -> 0; matrix products, arithmetic and copies ran while one was open for 9% -> 0% of each run, Pallas kernels for 0% -> 0%
where the time goes in v2:
time: 78.9 us; the launch traced here: 78.8 us
  Pallas kernels  72.2 us (92%)
  other arithmetic  3.81 us (5%)
  local copies, waits for them, and re-layouts  2.05 us (3%)
    pallas_call x1, Pallas kernels, shards(): pl.pallas_call(body, out_shape=(jax.ShapeDtypeStruct(frames.shape, jnp.bf...  72.2 us
    convert_element_type x1, other arithmetic, f32(): return value.astype(jnp.float32)  3.81 us
    unnamed x9, local copies, waits for them, and re-layouts  2.05 us

profile of v2, /device:TPU:1, one launch (start us, length us, event | category | flops | bytes accessed | tf_op | source)
XLA Modules:
  0.0 78.8 jit_solution(5343368627475571972)
XLA Ops:
  0.6 72.2 %shard_map.126 = (bf16[2,128,512]{2,1,0:T(8,128)(2,1)}, bf16[2,128,512]{2,1,0:T(8,128)(2,1)}, f32[31,512]{1,0:T(8,128)}, bf16[4,512,512]{2,1,0:T(8,128)(2,1)}) custom-call(bf16[2,128,512]{2,1,0:T(8,128)(2,1)} %refs_0_.1, bf16[2,128,512]{2,1,0:T(8,128)(2,1)} %refs_1_.1, f32[31,512]{1,0:T(8,128)} %refs_2_.1, bf16[512,512]{1,0:T(8,128)(2,1)} %refs_3_.1, ...), custom_call_target="tpu_custom_call" | custom-call | tf_op jit(solution)/shard_map/pallas_call | solution.py:619
  72.9 0.0 copy-start.1
  72.9 0.0 copy-start
  72.9 0.0 copy-start.2
  72.9 3.8 %bitcast_convert_fusion = (f32[512,512]{1,0:T(8,128)}, f32[512,512]{1,0:T(8,128)}, f32[512,512]{1,0:T(8,128)}, f32[512,512]{1,0:T(8,128)}) fusion(bf16[4,512,512]{2,1,0:T(8,128)(2,1)} %get-tuple-element.14), kind=kLoop, calls=%fused_computation | loop fusion | flops 1048576 | bytes 6291456 | tf_op jit(solution)/shard_map/convert_element_type | solution.py:73
  76.7 0.0 copy-done.1
  76.7 0.7 copy.17
  77.4 0.0 copy-done
  77.4 0.7 copy.18
  78.1 0.0 copy-done.2
  78.1 0.6 copy.19
Async XLA Ops:
  72.9 3.8 %copy-start.1 = (bf16[2,128,512]{2,1,0:T(8,128)(2,1)S(1)}, bf16[2,128,512]{2,1,0:T(8,128)(2,1)}, u32[]{:S(2)}) copy-start(bf16[2,128,512]{2,1,0:T(8,128)(2,1)} %get-tuple-element.26) | copy-start | bytes 786436
  72.9 4.5 %copy-start = (bf16[2,128,512]{2,1,0:T(8,128)(2,1)S(1)}, bf16[2,128,512]{2,1,0:T(8,128)(2,1)}, u32[]{:S(2)}) copy-start(bf16[2,128,512]{2,1,0:T(8,128)(2,1)} %get-tuple-element.27) | copy-start | bytes 786436
  72.9 5.2 %copy-start.2 = (f32[31,512]{1,0:T(8,128)S(1)}, f32[31,512]{1,0:T(8,128)}, u32[]{:S(2)}) copy-start(f32[31,512]{1,0:T(8,128)} %get-tuple-element.28) | copy-start | bytes 190468

commit v3 on v2

v3 whole, which is shorter than its diff:
```python
import math
import types

import jax
import jax.numpy as jnp
from jax import lax
from jax.experimental import pallas as pl
from jax.experimental.pallas import tpu as pltpu
from jax.sharding import PartitionSpec as P

HEADS = 8
FRAMES = 128
SHARE = 32
NX, NY, NZ = 4, 4, 8
MESH = pl.DeviceIdType.MESH


class Place:
    def __init__(self):
        mic = lax.axis_index("mic")
        tm = lax.axis_index("tm")
        self.mic, self.tm = mic, tm
        self.core = lax.rem(mic, 2)
        self.x = lax.rem(tm, NX)
        self.z = lax.rem(lax.div(tm, NX), NZ)
        self.y = lax.div(tm, NX * NZ) * 2 + lax.div(mic, 2)

    def device(self, x=None, y=None, z=None, core=None):
        x = self.x if x is None else x
        y = self.y if y is None else y
        z = self.z if z is None else z
        core = self.core if core is None else core
        mic = lax.rem(y, 2) * 2 + core
        tm = lax.div(y, 2) * (NX * NZ) + z * NX + x
        return (mic, tm)

    def along(self, axis, step):
        size = {"x": NX, "y": NY, "z": NZ, "core": 2}[axis]
        index = lax.rem(getattr(self, axis) + step, size)
        return index, self.device(**{axis: index})


def rows_at(start, count):
    return pl.ds(pl.multiple_of(start, count), count)


def send(src, dst, send_sem, recv_sem, device):
    copy = pltpu.make_async_remote_copy(
        src_ref=src,
        dst_ref=dst,
        send_sem=send_sem,
        recv_sem=recv_sem,
        device_id=device,
        device_id_type=MESH,
    )
    copy.start()
    return copy


def local(src, dst, sem):
    copy = pltpu.make_async_copy(src, dst, sem)
    copy.start()
    return copy


SIZES = {"x": NX, "y": NY, "z": NZ, "core": 2}
HALF, STREAM, FIRST, SECOND, TILE = 4096, 2048, 512, 128, 16
ORDERS = (("x", "y", "z"), ("y", "x", "z"))


ACT, ACT_S, MIXED, DQUERY, DKEY, DVALUE, COT, COT_S, FIRST_S, SECOND_S = range(10)


def f32(value):
    return value.astype(jnp.float32)


def dot(left, right, left_dim=1, right_dim=0):
    return lax.dot_general(
        left, right, (((left_dim,), (right_dim,)), ((), ())), preferred_element_type=jnp.float32
    )


def lanes(block):
    return pl.ds(pl.multiple_of(block * 128, 128), 128)


def shifted(padded, mic, block, base, count):
    for offset in range(1, 32):
        yield offset, padded[mic, block, base + offset : base + offset + count]


def kernel_body(
    scale,
    frames,
    cotangent,
    taps,
    w_query,
    w_key,
    w_value,
    w_out,
    layer_out,
    frame_grad,
    tap_out,
    grads_out,
    m,
):
    bf16 = jnp.bfloat16
    here = Place()
    width = frames.shape[2]
    rows = 8 * SHARE
    count = NX * NY * NZ // 2
    group = [lax.rem(here.mic + step, 4) for step in range(1, 4)]
    after = (here.mic, lax.rem(here.tm + 1, count))
    before = (here.mic, lax.rem(here.tm + count - 1, count))
    peers = [after, before]
    peers += [(mic, here.tm) for mic in group]
    for axis in ("core", "x", "y", "z"):
        for step in range(1, SIZES[axis]):
            peers.append(here.along(axis, step)[1])
    barrier = pltpu.get_barrier_semaphore()
    for peer in peers:
        pl.semaphore_signal(barrier, inc=1, device_id=peer, device_id_type=MESH)
    loads = {}
    for at, (name, source) in enumerate(
        (
            ("frames", frames),
            ("taps", taps),
            ("cot", cotangent),
            ("w_out", w_out),
            ("w_query", w_query),
            ("w_key", w_key),
            ("w_value", w_value),
        )
    ):
        loads[name] = local(source, getattr(m, name), m.load.at[at])
    pl.semaphore_wait(barrier, len(peers))
    sent = []

    halo = [
        send(frames.at[:, pl.ds(FRAMES - 16, 16), :], m.halo.at[0], m.hs.at[0], m.hr.at[0], after),
        send(frames.at[:, pl.ds(0, 16), :], m.halo.at[1], m.hs.at[1], m.hr.at[1], before),
    ]
    mics_here = pl.ds(here.mic * 2, 2)
    share_here = rows_at(here.mic * SHARE, SHARE)
    cot_copies = []
    for step, mic in enumerate(group):
        cot_copies.append(
            send(
                cotangent.at[:, rows_at(mic * SHARE, SHARE), :],
                m.pool.at[COT, mics_here],
                m.cs.at[step],
                m.cr.at[step],
                (mic, here.tm),
            )
        )
    sent += halo + cot_copies
    loads["frames"].wait()
    loads["taps"].wait()
    for block in range(4):
        m.taps4[block, 0:31] = m.taps[:, block * 128 : (block + 1) * 128]
        for mic in range(2):
            m.fpad[mic, block, 16 : 16 + FRAMES] = f32(
                m.frames[mic, :, block * 128 : (block + 1) * 128]
            )

    def conv_rows(mic, block, base, number):
        conv = jnp.zeros((number, 128), jnp.float32)
        for offset, part in shifted(m.fpad, mic, block, base, number):
            conv = conv + part * m.taps4[block, offset - 1 : offset]
        sig = 1.0 / (1.0 + jnp.exp(-conv))
        m.acted[mic, base : base + number, lanes(block)] = (conv * sig).astype(bf16)
        m.dsilu[mic, block, base : base + number] = sig * (1.0 + conv * (1.0 - sig))

    def inner_block(step, carry):
        conv_rows(lax.div(step, 4), lax.rem(step, 4), 16, FRAMES - 32)
        return carry

    lax.fori_loop(0, 8, inner_block, 0)

    row = lax.broadcasted_iota(jnp.int32, (512, 128), 0)
    col = lax.broadcasted_iota(jnp.int32, (512, 128), 1)
    m.gather_heads[...] = jnp.where(lax.div(row, 64) == col, 1.0, 0.0).astype(bf16)
    row = lax.broadcasted_iota(jnp.int32, (128, 512), 0)
    col = lax.broadcasted_iota(jnp.int32, (128, 512), 1)
    m.spread_heads[...] = jnp.where(lax.div(col, 64) == row, 1.0, 0.0).astype(bf16)
    loads["cot"].wait()
    m.pool[COT, mics_here] = m.cot[:, share_here, :]

    def fill_halo(side, pad, buffer, copy):
        copy.wait_recv()
        inside = here.tm > 0 if side == 0 else here.tm < count - 1
        place = slice(0, 16) if side == 0 else slice(16 + FRAMES, 32 + FRAMES)
        for mic in range(2):
            for block in range(4):
                value = f32(buffer[side, mic, :, block * 128 : (block + 1) * 128])
                pad[mic, block, place] = jnp.where(inside, value, 0.0)

    for side in range(2):
        fill_halo(side, m.fpad, m.halo, halo[side])

    act_copies = []
    for mic in range(2):

        def outer_block(block, carry):
            conv_rows(mic, block, 0, 16)
            conv_rows(mic, block, FRAMES - 16, 16)
            return carry

        lax.fori_loop(0, 4, outer_block, 0)
        for step, target in enumerate(group):
            act_copies.append(
                send(
                    m.acted.at[mic, rows_at(target * SHARE, SHARE), :],
                    m.pool.at[ACT, here.mic * 2 + mic],
                    m.acs.at[mic, step],
                    m.acr.at[mic, step],
                    (target, here.tm),
                )
            )
        m.pool[ACT, here.mic * 2 + mic] = m.acted[mic, share_here, :]
    sent += act_copies

    other, sibling = here.along("core", 1)

    def to_sibling(source, target):
        copy = send(
            m.pool.at[source],
            m.pool.at[target],
            m.core_s.at[target],
            m.core_r.at[target],
            sibling,
        )
        sent.append(copy)
        return copy

    for copy in cot_copies:
        copy.wait_recv()
    shared = {COT_S: to_sibling(COT, COT_S)}
    cot_rows = m.pool[COT].reshape(rows, width)
    loads["w_out"].wait()
    m.ups[...] = dot(cot_rows, m.w_out[...], 1, 1).astype(bf16).reshape(8, SHARE, width)
    for name in ("w_query", "w_key", "w_value"):
        loads[name].wait()
    for copy in act_copies:
        copy.wait_recv()
    shared[ACT_S] = to_sibling(ACT, ACT_S)
    act_rows = m.pool[ACT].reshape(rows, width)
    for weight, target in ((m.w_query, m.queries), (m.w_key, m.keys), (m.w_value, m.values)):
        target[...] = dot(act_rows, weight[...]).astype(bf16).reshape(8, SHARE, width)

    m.dkey[...] = jnp.zeros_like(m.dkey)
    m.dvalue[...] = jnp.zeros_like(m.dvalue)
    factor = 1.0 / math.sqrt(width // HEADS)

    def attend(index, carry):
        query, up = m.queries[index], m.ups[index]
        keys, values = m.keys[...], m.values[...]
        gather, spread = m.gather_heads[...], m.spread_heads[...]

        def per_head(product):
            return dot(product.reshape(rows, width), gather).reshape(8, SHARE, 128)

        def per_lane(heads):
            return dot(heads.astype(bf16).reshape(rows, 128), spread).reshape(8, SHARE, width)

        weights = jnp.exp(per_head(query[None] * keys) * factor)
        weights = weights / jnp.sum(weights, axis=0, keepdims=True)
        products = per_head(up[None] * values)
        inner = weights * (products - jnp.sum(weights * products, axis=0, keepdims=True)) * factor
        weights, inner = per_lane(weights), per_lane(inner)
        m.pool[MIXED, index] = jnp.sum(weights * f32(values), axis=0).astype(bf16)
        m.pool[DQUERY, index] = jnp.sum(inner * f32(keys), axis=0).astype(bf16)
        m.dkey[...] += inner * f32(query)[None]
        m.dvalue[...] += weights * f32(up)[None]
        return carry

    lax.fori_loop(0, 8, attend, 0)

    shared[FIRST_S] = to_sibling(DQUERY - other, FIRST_S)
    m.pool[DKEY] = m.dkey[...].astype(bf16)
    m.pool[DVALUE] = m.dvalue[...].astype(bf16)
    shared[SECOND_S] = to_sibling(DKEY + other, SECOND_S)

    def pooled(index):
        return m.pool[index].reshape(rows, width)

    dacted = dot(pooled(DQUERY), m.w_query[...], 1, 1)
    dacted = dacted + dot(pooled(DKEY), m.w_key[...], 1, 1)
    dacted = dacted + dot(pooled(DVALUE), m.w_value[...], 1, 1)
    m.dacted[...] = dacted.astype(bf16).reshape(8, SHARE, width)
    def send_home(kind, source, target):
        copies = []
        for step, mic in enumerate(group):
            copies.append(
                send(
                    source.at[pl.ds(mic * 2, 2)],
                    target.at[:, share_here, :],
                    m.bs.at[kind, step],
                    m.br.at[kind, step],
                    (mic, here.tm),
                )
            )
        target[:, share_here, :] = source[mics_here]
        sent.extend(copies)
        return copies

    dacted_copies = send_home(0, m.dacted, m.dacted_home)

    core = here.core
    operands = (
        ((ACT, DQUERY + 2 * core), (ACT_S, FIRST_S + core)),
        ((2 * core, DKEY + 2 * core), (ACT_S + 7 * core, SECOND_S - 2 * core)),
    )
    terms = []
    for mine, _ in operands:
        terms.append(dot(pooled(mine[0]), pooled(mine[1]), 0, 0))
    for copy in shared.values():
        copy.wait_recv()
    first = []
    for s in range(2):
        _, theirs = operands[s]
        term = (terms[s] + dot(pooled(theirs[0]), pooled(theirs[1]), 0, 0)).astype(bf16)
        for block in range(4):
            at = s * STREAM + block * 512
            m.mine[at : at + 512, :] = term[:, block * 128 : (block + 1) * 128]
        axis = ORDERS[s][0]
        copies = []
        for step in (2, 1, 3):
            index, peer = here.along(axis, step)
            copies.append(
                send(
                    m.mine.at[rows_at(s * STREAM + index * FIRST, FIRST)],
                    m.rx1.at[s, step - 1],
                    m.s1.at[s, step - 1],
                    m.r1.at[s, step - 1],
                    peer,
                )
            )
        first.append(copies)
        sent += copies

    mixed_copies = send_home(1, m.pool.at[MIXED], m.mixed_home)

    for copy in dacted_copies:
        copy.wait_recv()

    def dconv_block(step, carry):
        mic, block = lax.div(step, 4), lax.rem(step, 4)
        dconv = f32(m.dacted_home[mic, :, lanes(block)]) * m.dsilu[mic, block]
        m.gpad[mic, block, 16 : 16 + FRAMES] = dconv
        m.ends[0, mic, :, lanes(block)] = dconv[FRAMES - 16 :].astype(bf16)
        m.ends[1, mic, :, lanes(block)] = dconv[:16].astype(bf16)
        return carry

    lax.fori_loop(0, 8, dconv_block, 0)
    ghalo = [
        send(m.ends.at[0], m.ghalo.at[0], m.hs.at[2], m.hr.at[2], after),
        send(m.ends.at[1], m.ghalo.at[1], m.hs.at[3], m.hr.at[3], before),
    ]
    sent += ghalo

    def tap_block(block, carry):
        sums = {}
        for mic in range(2):
            dconv = m.gpad[mic, block, 16 : 16 + FRAMES]
            for offset, part in shifted(m.fpad, mic, block, 0, FRAMES):
                part = jnp.sum((part * dconv).reshape(FRAMES // 8, 8, 128), axis=0)
                sums[offset] = sums[offset] + part if mic else part
        for offset, part in sums.items():
            m.tap0[block, offset - 1 : offset] = jnp.sum(part, axis=0, keepdims=True)
        m.tap0[block, 31:32] = jnp.zeros((1, 128), jnp.float32)
        return carry

    lax.fori_loop(0, 4, tap_block, 0)

    def tap_tile(index):
        return lax.div(index, 2), rows_at(lax.rem(index, 2) * 16, 16)

    tap_copies = []
    for step in range(1, NZ):
        index, peer = here.along("z", step)
        block, part = tap_tile(index)
        tap_copies.append(
            send(
                m.tap0.at[block, part],
                m.tap_zrx.at[step - 1],
                m.ts.at[step - 1],
                m.tr.at[step - 1],
                peer,
            )
        )
    sent += tap_copies

    for side in range(2):
        fill_halo(side, m.gpad, m.ghalo, ghalo[side])

    def grad_block(step, carry):
        mic, block = lax.div(step, 4), lax.rem(step, 4)
        total = f32(m.cot[mic, :, lanes(block)])
        for offset, part in shifted(m.gpad, mic, block, 0, FRAMES):
            total = total + part * m.taps4[block, 31 - offset : 32 - offset]
        m.fgrad[mic, :, lanes(block)] = total.astype(bf16)
        return carry

    lax.fori_loop(0, 8, grad_block, 0)
    stores = [local(m.fgrad, frame_grad, m.store.at[1])]

    second = []
    for s in range(2):
        axis, axis2, _ = ORDERS[s]
        place = s * STREAM + getattr(here, axis) * FIRST
        for copy in first[s]:
            copy.wait_recv()
        part = rows_at(place, FIRST)
        total = f32(m.mine[part, :])
        for step in range(SIZES[axis] - 1):
            total = total + f32(m.rx1[s, step])
        m.mine[part, :] = total.astype(bf16)
        copies = []
        for step in (2, 1, 3):
            index, peer = here.along(axis2, step)
            copies.append(
                send(
                    m.mine.at[rows_at(place + index * SECOND, SECOND)],
                    m.rx2.at[s, step - 1],
                    m.s2.at[s, step - 1],
                    m.r2.at[s, step - 1],
                    peer,
                )
            )
        second.append((place, copies))
        sent += copies

    for copy in mixed_copies:
        copy.wait_recv()
    home_rows = m.mixed_home[...].reshape(2 * FRAMES, width)
    m.layer[...] = (
        f32(m.frames[...]) + dot(home_rows, m.w_out[...]).reshape(2, FRAMES, width)
    ).astype(bf16)
    stores.append(local(m.layer, layer_out, m.store.at[0]))

    block, part = tap_tile(here.z)
    total = m.tap0[block, part]
    for step in range(1, NZ):
        tap_copies[step - 1].wait_recv()
        total = total + m.tap_zrx[step - 1]

    def tap_axis(tile, axis, base):
        slot = base + getattr(here, axis)
        m.tap_rx[slot] = tile
        copies = []
        for step in range(1, SIZES[axis]):
            copies.append(
                send(
                    m.tap_rx.at[slot],
                    m.tap_rx.at[slot],
                    m.ts.at[NZ - 1 + base + step - 1],
                    m.tr.at[NZ - 1 + base + step - 1],
                    here.along(axis, step)[1],
                )
            )
        return copies

    def tap_sum(copies, base):
        for copy in copies:
            copy.wait_recv()
        total = m.tap_rx[base]
        for index in range(len(copies)):
            total = total + m.tap_rx[base + 1 + index]
        return total

    tap_x = tap_axis(total, "x", 0)
    sent += tap_x

    far_first = (4, 3, 5, 2, 6, 1, 7)
    third = []
    for s in range(2):
        axis2 = ORDERS[s][1]
        place, copies = second[s]
        place = place + getattr(here, axis2) * SECOND
        for copy in copies:
            copy.wait_recv()
        part = rows_at(place, SECOND)
        total = f32(m.mine[part, :])
        for step in range(SIZES[axis2] - 1):
            total = total + f32(m.rx2[s, step])
        m.mine[part, :] = total.astype(bf16)
        copies = []
        for step in far_first:
            index, peer = here.along("z", step)
            copies.append(
                send(
                    m.mine.at[rows_at(place + index * TILE, TILE)],
                    m.rx3.at[s, step - 1],
                    m.s3.at[s, step - 1],
                    m.r3.at[s, step - 1],
                    peer,
                )
            )
        third.append((place, copies))
        sent += copies

    tap_y = tap_axis(tap_sum(tap_x, 0), "y", 4)
    sent += tap_y

    def gather(s, level, axis, place, number):
        copies = {}
        base = (0, NZ - 1, NZ + 2)[level]
        part = rows_at(place, number)
        for step in far_first if level == 0 else (2, 1, 3):
            copies[step] = send(
                m.full.at[part],
                m.full.at[part],
                m.gs.at[s, base + step - 1],
                m.gr.at[s, base + step - 1],
                here.along(axis, step)[1],
            )
        return copies

    back = []
    for s in range(2):
        place, copies = third[s]
        for copy in copies:
            copy.wait_recv()
        part = rows_at(place + here.z * TILE, TILE)
        total = f32(m.mine[part, :])
        for step in range(NZ - 1):
            total = total + f32(m.rx3[s, step])
        m.full[part, :] = (total * scale).astype(bf16)
        copies = gather(s, 0, "z", place + here.z * TILE, TILE)
        back.append((place, copies))
        sent += copies.values()

    tap_c = tap_axis(tap_sum(tap_y, 4), "core", 8)
    sent += tap_c

    last = []

    def finished(s, slot, place):
        part, out = rows_at(place, FIRST), rows_at(core * HALF + place, FIRST)
        stores.append(local(m.full.at[part], grads_out.at[out], m.store.at[3 + s * 4 + slot]))
        last.append(
            send(
                m.full.at[part],
                grads_out.at[out],
                m.gcs.at[s, slot],
                m.gcr.at[s, slot],
                sibling,
            )
        )

    for level in (1, 2):
        for s in range(2):
            place, copies = back[s]
            for copy in copies.values():
                copy.wait_recv()
            axis = ORDERS[s][2 - level]
            number = (TILE, SECOND, FIRST)[level]
            copies = gather(s, level, axis, place, number)
            sent += copies.values()
            if level == 2:
                finished(s, 0, place)
            back[s] = (place - getattr(here, axis) * number, copies)
        if level == 1:
            block, part = tap_tile(here.z)
            m.tap_full[block, part] = tap_sum(tap_c, 8) * scale
            tap_back = []
            for step in far_first:
                tap_back.append(
                    send(
                        m.tap_full.at[block, part],
                        m.tap_full.at[block, part],
                        m.tgs.at[step - 1],
                        m.tgr.at[step - 1],
                        here.along("z", step)[1],
                    )
                )
            sent += tap_back
    for copy in tap_back:
        copy.wait_recv()
    for block in range(4):
        m.tap_sum[:, block * 128 : (block + 1) * 128] = m.tap_full[block, 0:31]
    stores.append(local(m.tap_sum, tap_out, m.store.at[2]))
    for copy in sent:
        copy.wait_send()
    for slot, step in enumerate((1, 3, 2)):
        for s in range(2):
            place, copies = back[s]
            copies[step].wait_recv()
            axis = ORDERS[s][0]
            size = SIZES[axis]
            index = lax.rem(getattr(here, axis) + size - step, size)
            finished(s, slot + 1, place + index * FIRST)
    for copy in stores:
        copy.wait()
    for copy in last:
        copy.wait_send()
        copy.wait_recv()


def memory(width):
    bf16, full = jnp.bfloat16, jnp.float32
    dma = pltpu.SemaphoreType.DMA
    rows = (8, SHARE, width)
    home = (2, FRAMES, width)
    wide = (2, 4, FRAMES + 32, 128)
    square = pltpu.VMEM((width, width), bf16)
    return dict(
        frames=pltpu.VMEM(home, bf16),
        cot=pltpu.VMEM(home, bf16),
        taps=pltpu.VMEM((31, width), full),
        w_query=square,
        w_key=square,
        w_value=square,
        w_out=square,
        layer=pltpu.VMEM(home, bf16),
        fgrad=pltpu.VMEM(home, bf16),
        tap_sum=pltpu.VMEM((31, width), full),
        halo=pltpu.VMEM((2, 2, 16, width), bf16),
        ghalo=pltpu.VMEM((2, 2, 16, width), bf16),
        ends=pltpu.VMEM((2, 2, 16, width), bf16),
        pool=pltpu.VMEM((10,) + rows, bf16),
        acted=pltpu.VMEM(home, bf16),
        taps4=pltpu.VMEM((4, 32, 128), full),
        fpad=pltpu.VMEM(wide, full),
        gpad=pltpu.VMEM(wide, full),
        dsilu=pltpu.VMEM((2, 4, FRAMES, 128), full),
        gather_heads=pltpu.VMEM((width, 128), bf16),
        spread_heads=pltpu.VMEM((128, width), bf16),
        queries=pltpu.VMEM(rows, bf16),
        keys=pltpu.VMEM(rows, bf16),
        values=pltpu.VMEM(rows, bf16),
        ups=pltpu.VMEM(rows, bf16),
        dkey=pltpu.VMEM(rows, full),
        dvalue=pltpu.VMEM(rows, full),
        dacted=pltpu.VMEM(rows, bf16),
        dacted_home=pltpu.VMEM(home, bf16),
        mixed_home=pltpu.VMEM(home, bf16),
        mine=pltpu.VMEM((HALF, 128), bf16),
        full=pltpu.VMEM((HALF, 128), bf16),
        rx1=pltpu.VMEM((2, 3, FIRST, 128), bf16),
        rx2=pltpu.VMEM((2, 3, SECOND, 128), bf16),
        rx3=pltpu.VMEM((2, NZ - 1, TILE, 128), bf16),
        tap0=pltpu.VMEM((4, 32, 128), full),
        tap_zrx=pltpu.VMEM((NZ - 1, 16, 128), full),
        tap_rx=pltpu.VMEM((10, 16, 128), full),
        tap_full=pltpu.VMEM((4, 32, 128), full),
        load=dma((7,)),
        store=dma((11,)),
        hs=dma((4,)),
        hr=dma((4,)),
        cs=dma((3,)),
        cr=dma((3,)),
        acs=dma((2, 3)),
        acr=dma((2, 3)),
        bs=dma((2, 3)),
        br=dma((2, 3)),
        core_s=dma((10,)),
        core_r=dma((10,)),
        s1=dma((2, 3)),
        r1=dma((2, 3)),
        s2=dma((2, 3)),
        r2=dma((2, 3)),
        s3=dma((2, NZ - 1)),
        r3=dma((2, NZ - 1)),
        gs=dma((2, NZ + 5)),
        gr=dma((2, NZ + 5)),
        gcs=dma((2, 4)),
        gcr=dma((2, 4)),
        ts=dma((NZ + 8,)),
        tr=dma((NZ + 8,)),
        tgs=dma((NZ - 1,)),
        tgr=dma((NZ - 1,)),
    )


def finish_body(layer, fgrad, taps, grads, layer_out, frame_grad, tap_out, *rest):
    outs, (packed, whole, held, held_taps, load, store) = rest[:4], rest[4:]
    loads = [local(grads.at[pl.ds(g * 2048, 2048)], packed.at[g], load.at[g]) for g in range(4)]
    small = ((layer, held.at[0], layer_out), (fgrad, held.at[1], frame_grad))
    small += ((taps, held_taps, tap_out),)
    first = [local(src, via, load.at[4 + at]) for at, (src, via, _) in enumerate(small)]
    moved = []
    for at, (_, via, dst) in enumerate(small):
        first[at].wait()
        moved.append(local(via, dst, store.at[4 + at]))
    for g in range(4):
        loads[g].wait()
        for block in range(4):
            whole[g, :, block * 128 : (block + 1) * 128] = f32(
                packed[g, block * 512 : (block + 1) * 512]
            )
        moved.append(local(whole.at[g], outs[g], store.at[g]))
    for copy in moved:
        copy.wait()


def shards(frames, cotangent, kernel, w_query, w_key, w_value, w_out):
    number, length, width = frames.shape
    scale = 1.0 / math.sqrt(lax.axis_size("mic") * number * lax.axis_size("tm") * length)
    scratch = memory(width)
    bf16, full = jnp.bfloat16, jnp.float32
    shape = jax.ShapeDtypeStruct
    outputs = (shape(frames.shape, bf16), shape(frames.shape, bf16), shape(kernel.shape, full))

    def body(*refs):
        parts = types.SimpleNamespace(**dict(zip(scratch, refs[11:])))
        kernel_body(scale, *refs[:11], parts)

    parts = pl.pallas_call(
        body,
        out_shape=outputs + (shape((2 * HALF, 128), bf16),),
        in_specs=[pl.BlockSpec(memory_space=pl.ANY)] * 7,
        out_specs=[pl.BlockSpec(memory_space=pl.ANY)] * 4,
        scratch_shapes=list(scratch.values()),
        compiler_params=pltpu.CompilerParams(
            collective_id=0, has_side_effects=True, vmem_limit_bytes=56 * 2**20
        ),
    )(frames, cotangent, kernel, w_query, w_key, w_value, w_out)
    dma = pltpu.SemaphoreType.DMA
    return pl.pallas_call(
        finish_body,
        out_shape=outputs + (shape((width, width), full),) * 4,
        in_specs=[pl.BlockSpec(memory_space=pl.ANY)] * 4,
        out_specs=[pl.BlockSpec(memory_space=pl.ANY)] * 7,
        scratch_shapes=[
            pltpu.VMEM((4, 2048, 128), bf16),
            pltpu.VMEM((4, width, width), full),
            pltpu.VMEM((2,) + frames.shape, bf16),
            pltpu.VMEM(kernel.shape, full),
            dma((7,)),
            dma((7,)),
        ],
        compiler_params=pltpu.CompilerParams(vmem_limit_bytes=56 * 2**20),
    )(*parts)


def solution(mesh):
    in_specs = (P("mic", "tm", None), P("mic", "tm", None), P(), P(), P(), P(), P())
    out_specs = (P("mic", "tm", None), P("mic", "tm", None), P(), P(), P(), P(), P())
    return jax.shard_map(shards, mesh=mesh, in_specs=in_specs, out_specs=out_specs, check_vma=False)
```

time: 78.9 us -> 71.5 us (0.906)
  other arithmetic: 3.81 us -> 0 us
  local copies, waits for them, and re-layouts: 2.05 us -> 0 us
  Pallas kernels: 72.2 us -> 70.7 us
    convert_element_type x1 -> x0, other arithmetic: 3.81 us -> none  [f32(): return value.astype(jnp.float32)]
    unnamed x9 -> x0, local copies, waits for them, and re-layouts: 2.05 us -> none
    pallas_call x1 -> x2, Pallas kernels: 72.2 us -> 70.7 us  [the longest x1 66.8 us: shards(): pl.pallas_call(body, out_shape=outputs + (shape((2 * HALF, 128), bf16),),...]
where the time goes in v3:
time: 71.5 us; the launch traced here: 71.3 us
  Pallas kernels  70.7 us (99%)
    pallas_call x1, Pallas kernels, shards(): pl.pallas_call(body, out_shape=outputs + (shape((2 * HALF, 128), bf16),),...  66.8 us
    pallas_call x1, Pallas kernels, shards(): pl.pallas_call(finish_body, out_shape=outputs + (shape((width, width), fu...  3.93 us

profile of v3, /device:TPU:1, one launch (start us, length us, event | category | flops | bytes accessed | tf_op | source)
XLA Modules:
  0.0 71.3 jit_solution(531215953089547930)
XLA Ops:
  0.6 66.8 %shard_map.126 = (bf16[2,128,512]{2,1,0:T(8,128)(2,1)}, bf16[2,128,512]{2,1,0:T(8,128)(2,1)}, f32[31,512]{1,0:T(8,128)}, bf16[8192,128]{1,0:T(8,128)(2,1)}) custom-call(bf16[2,128,512]{2,1,0:T(8,128)(2,1)} %refs_0_.1, bf16[2,128,512]{2,1,0:T(8,128)(2,1)} %refs_1_.1, f32[31,512]{1,0:T(8,128)} %refs_2_.1, bf16[512,512]{1,0:T(8,128)(2,1)} %refs_3_.1, ...), custom_call_target="tpu_custom_call" | custom-call | tf_op jit(solution)/shard_map/pallas_call | solution.py:711
  67.4 3.9 %shard_map.127 = (bf16[2,128,512]{2,1,0:T(8,128)(2,1)}, bf16[2,128,512]{2,1,0:T(8,128)(2,1)}, f32[31,512]{1,0:T(8,128)}, f32[512,512]{1,0:T(8,128)}, f32[512,512...) custom-call(bf16[2,128,512]{2,1,0:T(8,128)(2,1)} %get-tuple-element.11.layer, ...), custom_call_target="tpu_custom_call" | custom-call | tf_op jit(solution)/shard_map/pallas_call | solution.py:722

commit v4 on v3

--- a/solution.py
+++ b/solution.py
@@ -64,7 +64,7 @@
 
 
 SIZES = {"x": NX, "y": NY, "z": NZ, "core": 2}
-HALF, STREAM, FIRST, SECOND, TILE = 4096, 2048, 512, 128, 16
+SECOND, TILE = 128, 16
 ORDERS = (("x", "y", "z"), ("y", "x", "z"))
 
 
@@ -317,30 +317,25 @@
         terms.append(dot(pooled(mine[0]), pooled(mine[1]), 0, 0))
     for copy in shared.values():
         copy.wait_recv()
-    first = []
+    first = [{}, {}]
     for s in range(2):
         _, theirs = operands[s]
         term = (terms[s] + dot(pooled(theirs[0]), pooled(theirs[1]), 0, 0)).astype(bf16)
         for block in range(4):
-            at = s * STREAM + block * 512
-            m.mine[at : at + 512, :] = term[:, block * 128 : (block + 1) * 128]
-        axis = ORDERS[s][0]
-        copies = []
-        for step in (2, 1, 3):
-            index, peer = here.along(axis, step)
-            copies.append(
-                send(
-                    m.mine.at[rows_at(s * STREAM + index * FIRST, FIRST)],
-                    m.rx1.at[s, step - 1],
-                    m.s1.at[s, step - 1],
-                    m.r1.at[s, step - 1],
+            m.mine[s, block] = term[:, block * 128 : (block + 1) * 128].reshape(4, SECOND, 128)
+        axis, axis2, _ = ORDERS[s]
+        for far in (2, 1, 3, 0):
+            index2, _ = here.along(axis2, far)
+            for step in (2, 1, 3):
+                index, peer = here.along(axis, step)
+                first[s][far, step] = send(
+                    m.mine.at[s, index, index2],
+                    m.rx1.at[s, step - 1, far],
+                    m.s1.at[s, step - 1, far],
+                    m.r1.at[s, step - 1, far],
                     peer,
                 )
-            )
-        first.append(copies)
-        sent += copies
-
-    mixed_copies = send_home(1, m.pool.at[MIXED], m.mixed_home)
+        sent += first[s].values()
 
     for copy in dacted_copies:
         copy.wait_recv()
@@ -392,53 +387,26 @@
         )
     sent += tap_copies
 
-    for side in range(2):
-        fill_halo(side, m.gpad, m.ghalo, ghalo[side])
-
-    def grad_block(step, carry):
-        mic, block = lax.div(step, 4), lax.rem(step, 4)
-        total = f32(m.cot[mic, :, lanes(block)])
-        for offset, part in shifted(m.gpad, mic, block, 0, FRAMES):
-            total = total + part * m.taps4[block, 31 - offset : 32 - offset]
-        m.fgrad[mic, :, lanes(block)] = total.astype(bf16)
-        return carry
-
-    lax.fori_loop(0, 8, grad_block, 0)
-    stores = [local(m.fgrad, frame_grad, m.store.at[1])]
-
-    second = []
-    for s in range(2):
-        axis, axis2, _ = ORDERS[s]
-        place = s * STREAM + getattr(here, axis) * FIRST
-        for copy in first[s]:
-            copy.wait_recv()
-        part = rows_at(place, FIRST)
-        total = f32(m.mine[part, :])
-        for step in range(SIZES[axis] - 1):
-            total = total + f32(m.rx1[s, step])
-        m.mine[part, :] = total.astype(bf16)
-        copies = []
-        for step in (2, 1, 3):
-            index, peer = here.along(axis2, step)
-            copies.append(
-                send(
-                    m.mine.at[rows_at(place + index * SECOND, SECOND)],
-                    m.rx2.at[s, step - 1],
-                    m.s2.at[s, step - 1],
-                    m.r2.at[s, step - 1],
+    second = [{}, {}]
+    for far in (2, 1, 3, 0):
+        for s in range(2):
+            axis, axis2, _ = ORDERS[s]
+            index = getattr(here, axis)
+            index2, peer = here.along(axis2, far)
+            total = f32(m.mine[s, index, index2])
+            for step in (1, 2, 3):
+                first[s][far, step].wait_recv()
+                total = total + f32(m.rx1[s, step - 1, far])
+            m.mine[s, index, index2] = total.astype(bf16)
+            if far:
+                second[s][far] = send(
+                    m.mine.at[s, index, index2],
+                    m.rx2.at[s, far - 1],
+                    m.s2.at[s, far - 1],
+                    m.r2.at[s, far - 1],
                     peer,
                 )
-            )
-        second.append((place, copies))
-        sent += copies
-
-    for copy in mixed_copies:
-        copy.wait_recv()
-    home_rows = m.mixed_home[...].reshape(2 * FRAMES, width)
-    m.layer[...] = (
-        f32(m.frames[...]) + dot(home_rows, m.w_out[...]).reshape(2, FRAMES, width)
-    ).astype(bf16)
-    stores.append(local(m.layer, layer_out, m.store.at[0]))
+                sent.append(second[s][far])
 
     block, part = tap_tile(here.z)
     total = m.tap0[block, part]
@@ -473,110 +441,131 @@
     tap_x = tap_axis(total, "x", 0)
     sent += tap_x
 
+    for side in range(2):
+        fill_halo(side, m.gpad, m.ghalo, ghalo[side])
+
+    def grad_block(step, carry):
+        mic, block = lax.div(step, 4), lax.rem(step, 4)
+        total = f32(m.cot[mic, :, lanes(block)])
+        for offset, part in shifted(m.gpad, mic, block, 0, FRAMES):
+            total = total + part * m.taps4[block, 31 - offset : 32 - offset]
+        m.fgrad[mic, :, lanes(block)] = total.astype(bf16)
+        return carry
+
+    lax.fori_loop(0, 8, grad_block, 0)
+    stores = [local(m.fgrad, frame_grad, m.store.at[1])]
+
     far_first = (4, 3, 5, 2, 6, 1, 7)
     third = []
     for s in range(2):
-        axis2 = ORDERS[s][1]
-        place, copies = second[s]
-        place = place + getattr(here, axis2) * SECOND
-        for copy in copies:
-            copy.wait_recv()
-        part = rows_at(place, SECOND)
-        total = f32(m.mine[part, :])
-        for step in range(SIZES[axis2] - 1):
-            total = total + f32(m.rx2[s, step])
-        m.mine[part, :] = total.astype(bf16)
+        axis, axis2, _ = ORDERS[s]
+        block = (s, getattr(here, axis), getattr(here, axis2))
+        total = f32(m.mine[block])
+        for far in (1, 2, 3):
+            second[s][far].wait_recv()
+            total = total + f32(m.rx2[s, far - 1])
+        m.mine[block] = total.astype(bf16)
         copies = []
         for step in far_first:
             index, peer = here.along("z", step)
             copies.append(
                 send(
-                    m.mine.at[rows_at(place + index * TILE, TILE)],
+                    m.mine.at[block + (rows_at(index * TILE, TILE),)],
                     m.rx3.at[s, step - 1],
                     m.s3.at[s, step - 1],
                     m.r3.at[s, step - 1],
                     peer,
                 )
             )
-        third.append((place, copies))
+        third.append((block, copies))
         sent += copies
+    mixed_copies = send_home(1, m.pool.at[MIXED], m.mixed_home)
 
     tap_y = tap_axis(tap_sum(tap_x, 0), "y", 4)
     sent += tap_y
 
-    def gather(s, level, axis, place, number):
-        copies = {}
-        base = (0, NZ - 1, NZ + 2)[level]
-        part = rows_at(place, number)
-        for step in far_first if level == 0 else (2, 1, 3):
-            copies[step] = send(
-                m.full.at[part],
-                m.full.at[part],
-                m.gs.at[s, base + step - 1],
-                m.gr.at[s, base + step - 1],
-                here.along(axis, step)[1],
-            )
-        return copies
-
     back = []
     for s in range(2):
-        place, copies = third[s]
+        block, copies = third[s]
+        part = block + (rows_at(here.z * TILE, TILE),)
+        total = f32(m.mine[part])
         for copy in copies:
             copy.wait_recv()
-        part = rows_at(place + here.z * TILE, TILE)
-        total = f32(m.mine[part, :])
         for step in range(NZ - 1):
             total = total + f32(m.rx3[s, step])
-        m.full[part, :] = (total * scale).astype(bf16)
-        copies = gather(s, 0, "z", place + here.z * TILE, TILE)
-        back.append((place, copies))
-        sent += copies.values()
+        m.full[part] = (total * scale).astype(bf16)
+        copies = []
+        for step in far_first:
+            copies.append(
+                send(
+                    m.full.at[part],
+                    m.full.at[part],
+                    m.gs.at[s, step - 1],
+                    m.gr.at[s, step - 1],
+                    here.along("z", step)[1],
+                )
+            )
+        back.append(copies)
+        sent += copies
 
     tap_c = tap_axis(tap_sum(tap_y, 4), "core", 8)
     sent += tap_c
 
-    last = []
-
-    def finished(s, slot, place):
-        part, out = rows_at(place, FIRST), rows_at(core * HALF + place, FIRST)
-        stores.append(local(m.full.at[part], grads_out.at[out], m.store.at[3 + s * 4 + slot]))
-        last.append(
+    for copy in mixed_copies:
+        copy.wait_recv()
+    home_rows = m.mixed_home[...].reshape(2 * FRAMES, width)
+    m.layer[...] = (
+        f32(m.frames[...]) + dot(home_rows, m.w_out[...]).reshape(2, FRAMES, width)
+    ).astype(bf16)
+    stores.append(local(m.layer, layer_out, m.store.at[0]))
+
+    block, part = tap_tile(here.z)
+    m.tap_full[block, part] = tap_sum(tap_c, 8) * scale
+    tap_back = []
+    for step in far_first:
+        tap_back.append(
             send(
-                m.full.at[part],
-                grads_out.at[out],
-                m.gcs.at[s, slot],
-                m.gcr.at[s, slot],
-                sibling,
+                m.tap_full.at[block, part],
+                m.tap_full.at[block, part],
+                m.tgs.at[step - 1],
+                m.tgr.at[step - 1],
+                here.along("z", step)[1],
             )
         )
-
-    for level in (1, 2):
+    sent += tap_back
+
+    def pass_on(s, axis, block, kind):
+        copies = []
+        for step in (2, 1, 3):
+            copies.append(
+                send(
+                    m.full.at[block],
+                    m.full.at[block],
+                    m.gs.at[s, NZ - 1 + kind * 3 + step - 1],
+                    m.gr.at[s, NZ - 1 + kind * 3 + step - 1],
+                    here.along(axis, step)[1],
+                )
+            )
+        sent.extend(copies)
+        return copies
+
+    across, along = [], [{}, {}]
+    for s in range(2):
+        for copy in back[s]:
+            copy.wait_recv()
+        block, _ = third[s]
+        across.append(pass_on(s, ORDERS[s][1], block, 0))
+        along[s][0] = pass_on(s, ORDERS[s][0], block, 1)
+
+    def sender(axis, step):
+        return lax.rem(getattr(here, axis) + SIZES[axis] - step, SIZES[axis])
+
+    for at, step in ((1, 1), (2, 3), (0, 2)):
         for s in range(2):
-            place, copies = back[s]
-            for copy in copies.values():
-                copy.wait_recv()
-            axis = ORDERS[s][2 - level]
-            number = (TILE, SECOND, FIRST)[level]
-            copies = gather(s, level, axis, place, number)
-            sent += copies.values()
-            if level == 2:
-                finished(s, 0, place)
-            back[s] = (place - getattr(here, axis) * number, copies)
-        if level == 1:
-            block, part = tap_tile(here.z)
-            m.tap_full[block, part] = tap_sum(tap_c, 8) * scale
-            tap_back = []
-            for step in far_first:
-                tap_back.append(
-                    send(
-                        m.tap_full.at[block, part],
-                        m.tap_full.at[block, part],
-                        m.tgs.at[step - 1],
-                        m.tgr.at[step - 1],
-                        here.along("z", step)[1],
-                    )
-                )
-            sent += tap_back
+            axis, axis2, _ = ORDERS[s]
+            across[s][at].wait_recv()
+            block = (s, getattr(here, axis), sender(axis2, step))
+            along[s][step] = pass_on(s, axis, block, 1 + step)
     for copy in tap_back:
         copy.wait_recv()
     for block in range(4):
@@ -584,14 +573,16 @@
     stores.append(local(m.tap_sum, tap_out, m.store.at[2]))
     for copy in sent:
         copy.wait_send()
-    for slot, step in enumerate((1, 3, 2)):
+    last = []
+    for step in (0, 1, 3, 2):
         for s in range(2):
-            place, copies = back[s]
-            copies[step].wait_recv()
-            axis = ORDERS[s][0]
-            size = SIZES[axis]
-            index = lax.rem(getattr(here, axis) + size - step, size)
-            finished(s, slot + 1, place + index * FIRST)
+            for copy in along[s][step]:
+                copy.wait_recv()
+            index2 = sender(ORDERS[s][1], step)
+            source = m.full.at[s, :, index2]
+            target = grads_out.at[core, s, :, index2]
+            stores.append(local(source, target, m.store.at[3 + s * 4 + step]))
+            last.append(send(source, target, m.gcs.at[s, step], m.gcr.at[s, step], sibling))
     for copy in stores:
         copy.wait()
     for copy in last:
@@ -637,9 +628,9 @@
         dacted=pltpu.VMEM(rows, bf16),
         dacted_home=pltpu.VMEM(home, bf16),
         mixed_home=pltpu.VMEM(home, bf16),
-        mine=pltpu.VMEM((HALF, 128), bf16),
-        full=pltpu.VMEM((HALF, 128), bf16),
-        rx1=pltpu.VMEM((2, 3, FIRST, 128), bf16),
+        mine=pltpu.VMEM((2, 4, 4, SECOND, 128), bf16),
+        full=pltpu.VMEM((2, 4, 4, SECOND, 128), bf16),
+        rx1=pltpu.VMEM((2, 3, 4, SECOND, 128), bf16),
         rx2=pltpu.VMEM((2, 3, SECOND, 128), bf16),
         rx3=pltpu.VMEM((2, NZ - 1, TILE, 128), bf16),
         tap0=pltpu.VMEM((4, 32, 128), full),
@@ -658,14 +649,14 @@
         br=dma((2, 3)),
         core_s=dma((10,)),
         core_r=dma((10,)),
-        s1=dma((2, 3)),
-        r1=dma((2, 3)),
+        s1=dma((2, 3, 4)),
+        r1=dma((2, 3, 4)),
         s2=dma((2, 3)),
         r2=dma((2, 3)),
         s3=dma((2, NZ - 1)),
         r3=dma((2, NZ - 1)),
-        gs=dma((2, NZ + 5)),
-        gr=dma((2, NZ + 5)),
+        gs=dma((2, NZ + 14)),
+        gr=dma((2, NZ + 14)),
         gcs=dma((2, 4)),
         gcr=dma((2, 4)),
         ts=dma((NZ + 8,)),
@@ -677,21 +668,25 @@
 
 def finish_body(layer, fgrad, taps, grads, layer_out, frame_grad, tap_out, *rest):
     outs, (packed, whole, held, held_taps, load, store) = rest[:4], rest[4:]
-    loads = [local(grads.at[pl.ds(g * 2048, 2048)], packed.at[g], load.at[g]) for g in range(4)]
+    chunks = [(g, half) for g in range(4) for half in range(2)]
+    loads = []
+    for at, (g, half) in enumerate(chunks):
+        part = grads.at[g // 2, g % 2, :, pl.ds(half * 2, 2)]
+        loads.append(local(part, packed.at[g, half], load.at[at]))
     small = ((layer, held.at[0], layer_out), (fgrad, held.at[1], frame_grad))
     small += ((taps, held_taps, tap_out),)
-    first = [local(src, via, load.at[4 + at]) for at, (src, via, _) in enumerate(small)]
+    first = [local(src, via, load.at[8 + at]) for at, (src, via, _) in enumerate(small)]
     moved = []
+    for at, (g, half) in enumerate(chunks):
+        loads[at].wait()
+        rows = pl.ds(half * 256, 256)
+        for block in range(4):
+            value = f32(packed[g, half, block]).reshape(256, 128)
+            whole[g, rows, block * 128 : (block + 1) * 128] = value
+        moved.append(local(whole.at[g, rows], outs[g].at[rows], store.at[at]))
     for at, (_, via, dst) in enumerate(small):
         first[at].wait()
-        moved.append(local(via, dst, store.at[4 + at]))
-    for g in range(4):
-        loads[g].wait()
-        for block in range(4):
-            whole[g, :, block * 128 : (block + 1) * 128] = f32(
-                packed[g, block * 512 : (block + 1) * 512]
-            )
-        moved.append(local(whole.at[g], outs[g], store.at[g]))
+        moved.append(local(via, dst, store.at[8 + at]))
     for copy in moved:
         copy.wait()
 
@@ -710,7 +705,7 @@
 
     parts = pl.pallas_call(
         body,
-        out_shape=outputs + (shape((2 * HALF, 128), bf16),),
+        out_shape=outputs + (shape((2, 2, 4, 4, SECOND, 128), bf16),),
         in_specs=[pl.BlockSpec(memory_space=pl.ANY)] * 7,
         out_specs=[pl.BlockSpec(memory_space=pl.ANY)] * 4,
         scratch_shapes=list(scratch.values()),
@@ -725,12 +720,12 @@
         in_specs=[pl.BlockSpec(memory_space=pl.ANY)] * 4,
         out_specs=[pl.BlockSpec(memory_space=pl.ANY)] * 7,
         scratch_shapes=[
-            pltpu.VMEM((4, 2048, 128), bf16),
+            pltpu.VMEM((4, 2, 4, 2, SECOND, 128), bf16),
             pltpu.VMEM((4, width, width), full),
             pltpu.VMEM((2,) + frames.shape, bf16),
             pltpu.VMEM(kernel.shape, full),
-            dma((7,)),
-            dma((7,)),
+            dma((11,)),
+            dma((11,)),
         ],
         compiler_params=pltpu.CompilerParams(vmem_limit_bytes=56 * 2**20),
     )(*parts)

time: 71.5 us -> 68 us (0.951)
  Pallas kernels: 70.7 us -> 67.2 us
    pallas_call x1, Pallas kernels: 66.8 us -> 63.8 us  [shards(): pl.pallas_call(body, out_shape=outputs + (shape((2, 2, 4, 4, SECOND, 128)...]
where the time goes in v4:
time: 68 us; the launch traced here: 67.9 us
  Pallas kernels  67.2 us (99%)
    pallas_call x1, Pallas kernels, shards(): pl.pallas_call(body, out_shape=outputs + (shape((2, 2, 4, 4, SECOND, 128)...  63.8 us
    pallas_call x1, Pallas kernels, shards(): pl.pallas_call(finish_body, out_shape=outputs + (shape((width, width), fu...  3.37 us

profile of v4, /device:TPU:1, one launch (start us, length us, event | category | flops | bytes accessed | tf_op | source)
XLA Modules:
  0.0 67.9 jit_solution(5674077442017526922)
XLA Ops:
  0.6 63.8 %shard_map.126 = (bf16[2,128,512]{2,1,0:T(8,128)(2,1)}, bf16[2,128,512]{2,1,0:T(8,128)(2,1)}, f32[31,512]{1,0:T(8,128)}, bf16[2,2,4,4,128,128]{5,4,3,2,1,0:T(8,128)(2,1)}) custom-call(bf16[2,128,512]{2,1,0:T(8,128)(2,1)} %refs_0_.1, bf16[2,128,512]{2,1,0:T(8,128)(2,1)} %refs_1_.1, f32[31,512]{1,0:T(8,128)} %refs_2_.1, bf16[512,512]{1,0:T(8,128)(2,1)} %refs_3_.1, ...), custom_call_target="tpu_custom_call" | custom-call | tf_op jit(solution)/shard_map/pallas_call | solution.py:706
  64.5 3.4 %shard_map.127 = (bf16[2,128,512]{2,1,0:T(8,128)(2,1)}, bf16[2,128,512]{2,1,0:T(8,128)(2,1)}, f32[31,512]{1,0:T(8,128)}, f32[512,512]{1,0:T(8,128)}, f32[512,512...) custom-call(bf16[2,128,512]{2,1,0:T(8,128)(2,1)} %get-tuple-element.11.layer, ...), custom_call_target="tpu_custom_call" | custom-call | tf_op jit(solution)/shard_map/pallas_call | solution.py:717

commit v5 on v4

--- a/solution.py
+++ b/solution.py
@@ -118,6 +118,8 @@
     for axis in ("core", "x", "y", "z"):
         for step in range(1, SIZES[axis]):
             peers.append(here.along(axis, step)[1])
+    over = [lax.rem(here.x + step, NX) for step in range(1, NX)]
+    peers += [here.device(x=x, core=1 - here.core) for x in over]
     barrier = pltpu.get_barrier_semaphore()
     for peer in peers:
         pl.semaphore_signal(barrier, inc=1, device_id=peer, device_id_type=MESH)
@@ -249,11 +251,9 @@
     for weight, target in ((m.w_query, m.queries), (m.w_key, m.keys), (m.w_value, m.values)):
         target[...] = dot(act_rows, weight[...]).astype(bf16).reshape(8, SHARE, width)
 
-    m.dkey[...] = jnp.zeros_like(m.dkey)
-    m.dvalue[...] = jnp.zeros_like(m.dvalue)
     factor = 1.0 / math.sqrt(width // HEADS)
 
-    def attend(index, carry):
+    def attend(index):
         query, up = m.queries[index], m.ups[index]
         keys, values = m.keys[...], m.values[...]
         gather, spread = m.gather_heads[...], m.spread_heads[...]
@@ -271,11 +271,26 @@
         weights, inner = per_lane(weights), per_lane(inner)
         m.pool[MIXED, index] = jnp.sum(weights * f32(values), axis=0).astype(bf16)
         m.pool[DQUERY, index] = jnp.sum(inner * f32(keys), axis=0).astype(bf16)
-        m.dkey[...] += inner * f32(query)[None]
-        m.dvalue[...] += weights * f32(up)[None]
+        return inner * f32(query)[None], weights * f32(up)[None]
+
+    def attend_two(step, carry):
+        dkey, dvalue = attend(2 * step)
+        dkey_too, dvalue_too = attend(2 * step + 1)
+        dkey, dvalue = dkey + dkey_too, dvalue + dvalue_too
+
+        @pl.when(step == 0)
+        def _():
+            m.dkey[...] = dkey
+            m.dvalue[...] = dvalue
+
+        @pl.when(step > 0)
+        def _():
+            m.dkey[...] += dkey
+            m.dvalue[...] += dvalue
+
         return carry
 
-    lax.fori_loop(0, 8, attend, 0)
+    lax.fori_loop(0, 4, attend_two, 0)
 
     shared[FIRST_S] = to_sibling(DQUERY - other, FIRST_S)
     m.pool[DKEY] = m.dkey[...].astype(bf16)
@@ -408,53 +423,6 @@
                 )
                 sent.append(second[s][far])
 
-    block, part = tap_tile(here.z)
-    total = m.tap0[block, part]
-    for step in range(1, NZ):
-        tap_copies[step - 1].wait_recv()
-        total = total + m.tap_zrx[step - 1]
-
-    def tap_axis(tile, axis, base):
-        slot = base + getattr(here, axis)
-        m.tap_rx[slot] = tile
-        copies = []
-        for step in range(1, SIZES[axis]):
-            copies.append(
-                send(
-                    m.tap_rx.at[slot],
-                    m.tap_rx.at[slot],
-                    m.ts.at[NZ - 1 + base + step - 1],
-                    m.tr.at[NZ - 1 + base + step - 1],
-                    here.along(axis, step)[1],
-                )
-            )
-        return copies
-
-    def tap_sum(copies, base):
-        for copy in copies:
-            copy.wait_recv()
-        total = m.tap_rx[base]
-        for index in range(len(copies)):
-            total = total + m.tap_rx[base + 1 + index]
-        return total
-
-    tap_x = tap_axis(total, "x", 0)
-    sent += tap_x
-
-    for side in range(2):
-        fill_halo(side, m.gpad, m.ghalo, ghalo[side])
-
-    def grad_block(step, carry):
-        mic, block = lax.div(step, 4), lax.rem(step, 4)
-        total = f32(m.cot[mic, :, lanes(block)])
-        for offset, part in shifted(m.gpad, mic, block, 0, FRAMES):
-            total = total + part * m.taps4[block, 31 - offset : 32 - offset]
-        m.fgrad[mic, :, lanes(block)] = total.astype(bf16)
-        return carry
-
-    lax.fori_loop(0, 8, grad_block, 0)
-    stores = [local(m.fgrad, frame_grad, m.store.at[1])]
-
     far_first = (4, 3, 5, 2, 6, 1, 7)
     third = []
     for s in range(2):
@@ -481,8 +449,47 @@
         sent += copies
     mixed_copies = send_home(1, m.pool.at[MIXED], m.mixed_home)
 
-    tap_y = tap_axis(tap_sum(tap_x, 0), "y", 4)
-    sent += tap_y
+    for side in range(2):
+        fill_halo(side, m.gpad, m.ghalo, ghalo[side])
+
+    def grad_block(step, carry):
+        mic, block = lax.div(step, 4), lax.rem(step, 4)
+        total = f32(m.cot[mic, :, lanes(block)])
+        for offset, part in shifted(m.gpad, mic, block, 0, FRAMES):
+            total = total + part * m.taps4[block, 31 - offset : 32 - offset]
+        m.fgrad[mic, :, lanes(block)] = total.astype(bf16)
+        return carry
+
+    lax.fori_loop(0, 8, grad_block, 0)
+    stores = [local(m.fgrad, frame_grad, m.store.at[1])]
+
+    block, part = tap_tile(here.z)
+    total = m.tap0[block, part]
+    for step in range(1, NZ):
+        tap_copies[step - 1].wait_recv()
+        total = total + m.tap_zrx[step - 1]
+
+    def tap_share(tile, slot, base, others):
+        m.tap_rx[slot] = tile
+        copies = []
+        for at, peer in enumerate(others):
+            copies.append(
+                send(m.tap_rx.at[slot], m.tap_rx.at[slot], m.ts.at[base + at], m.tr.at[base + at], peer)
+            )
+        return copies
+
+    def tap_sum(copies, base):
+        for copy in copies:
+            copy.wait_recv()
+        total = m.tap_rx[base]
+        for index in range(len(copies)):
+            total = total + m.tap_rx[base + 1 + index]
+        return total
+
+    others = [here.device(x=x, core=core) for x in over for core in (here.core, 1 - here.core)]
+    others.append(sibling)
+    tap_x = tap_share(total, here.x * 2 + here.core, NZ - 1, others)
+    sent += tap_x
 
     back = []
     for s in range(2):
@@ -508,8 +515,9 @@
         back.append(copies)
         sent += copies
 
-    tap_c = tap_axis(tap_sum(tap_y, 4), "core", 8)
-    sent += tap_c
+    others = [here.along("y", step)[1] for step in (2, 1, 3)]
+    tap_y = tap_share(tap_sum(tap_x, 0), 8 + here.y, NZ + 6, others)
+    sent += tap_y
 
     for copy in mixed_copies:
         copy.wait_recv()
@@ -519,20 +527,7 @@
     ).astype(bf16)
     stores.append(local(m.layer, layer_out, m.store.at[0]))
 
-    block, part = tap_tile(here.z)
-    m.tap_full[block, part] = tap_sum(tap_c, 8) * scale
-    tap_back = []
-    for step in far_first:
-        tap_back.append(
-            send(
-                m.tap_full.at[block, part],
-                m.tap_full.at[block, part],
-                m.tgs.at[step - 1],
-                m.tgr.at[step - 1],
-                here.along("z", step)[1],
-            )
-        )
-    sent += tap_back
+    early, sent = sent, []
 
     def pass_on(s, axis, block, kind):
         copies = []
@@ -566,12 +561,22 @@
             across[s][at].wait_recv()
             block = (s, getattr(here, axis), sender(axis2, step))
             along[s][step] = pass_on(s, axis, block, 1 + step)
-    for copy in tap_back:
-        copy.wait_recv()
-    for block in range(4):
-        m.tap_sum[:, block * 128 : (block + 1) * 128] = m.tap_full[block, 0:31]
-    stores.append(local(m.tap_sum, tap_out, m.store.at[2]))
-    for copy in sent:
+    block, part = tap_tile(here.z)
+    m.tap_full[block, part] = tap_sum(tap_y, 8) * scale
+    tap_back = []
+    for step in far_first:
+        tap_back.append(
+            send(
+                m.tap_full.at[block, part],
+                m.tap_full.at[block, part],
+                m.tgs.at[step - 1],
+                m.tgr.at[step - 1],
+                here.along("z", step)[1],
+            )
+        )
+    sent += tap_back
+
+    for copy in early:
         copy.wait_send()
     last = []
     for step in (0, 1, 3, 2):
@@ -583,6 +588,13 @@
             target = grads_out.at[core, s, :, index2]
             stores.append(local(source, target, m.store.at[3 + s * 4 + step]))
             last.append(send(source, target, m.gcs.at[s, step], m.gcr.at[s, step], sibling))
+    for copy in tap_back:
+        copy.wait_recv()
+    for block in range(4):
+        m.tap_sum[:, block * 128 : (block + 1) * 128] = m.tap_full[block, 0:31]
+    stores.append(local(m.tap_sum, tap_out, m.store.at[2]))
+    for copy in sent:
+        copy.wait_send()
     for copy in stores:
         copy.wait()
     for copy in last:
@@ -635,7 +647,7 @@
         rx3=pltpu.VMEM((2, NZ - 1, TILE, 128), bf16),
         tap0=pltpu.VMEM((4, 32, 128), full),
         tap_zrx=pltpu.VMEM((NZ - 1, 16, 128), full),
-        tap_rx=pltpu.VMEM((10, 16, 128), full),
+        tap_rx=pltpu.VMEM((12, 16, 128), full),
         tap_full=pltpu.VMEM((4, 32, 128), full),
         load=dma((7,)),
         store=dma((11,)),
@@ -659,8 +671,8 @@
         gr=dma((2, NZ + 14)),
         gcs=dma((2, 4)),
         gcr=dma((2, 4)),
-        ts=dma((NZ + 8,)),
-        tr=dma((NZ + 8,)),
+        ts=dma((NZ + 9,)),
+        tr=dma((NZ + 9,)),
         tgs=dma((NZ - 1,)),
         tgr=dma((NZ - 1,)),
     )

time: 68 us -> 66.9 us (0.984)
  Pallas kernels: 67.2 us -> 66.2 us
    pallas_call x1, Pallas kernels: 63.8 us -> 62.8 us  [shards(): pl.pallas_call(body, out_shape=outputs + (shape((2, 2, 4, 4, SECOND, 128)...]
where the time goes in v5:
time: 66.9 us; the launch traced here: 66.8 us
  Pallas kernels  66.2 us (99%)
    pallas_call x1, Pallas kernels, shards(): pl.pallas_call(body, out_shape=outputs + (shape((2, 2, 4, 4, SECOND, 128)...  62.8 us
    pallas_call x1, Pallas kernels, shards(): pl.pallas_call(finish_body, out_shape=outputs + (shape((width, width), fu...  3.37 us

profile of v5, /device:TPU:1, one launch (start us, length us, event | category | flops | bytes accessed | tf_op | source)
XLA Modules:
  0.0 66.8 jit_solution(5284734552077841501)
XLA Ops:
  0.6 62.8 %shard_map.126 = (bf16[2,128,512]{2,1,0:T(8,128)(2,1)}, bf16[2,128,512]{2,1,0:T(8,128)(2,1)}, f32[31,512]{1,0:T(8,128)}, bf16[2,2,4,4,128,128]{5,4,3,2,1,0:T(8,128)(2,1)}) custom-call(bf16[2,128,512]{2,1,0:T(8,128)(2,1)} %refs_0_.1, bf16[2,128,512]{2,1,0:T(8,128)(2,1)} %refs_1_.1, f32[31,512]{1,0:T(8,128)} %refs_2_.1, bf16[512,512]{1,0:T(8,128)(2,1)} %refs_3_.1, ...), custom_call_target="tpu_custom_call" | custom-call | tf_op jit(solution)/shard_map/pallas_call | solution.py:718
  63.4 3.4 %shard_map.127 = (bf16[2,128,512]{2,1,0:T(8,128)(2,1)}, bf16[2,128,512]{2,1,0:T(8,128)(2,1)}, f32[31,512]{1,0:T(8,128)}, f32[512,512]{1,0:T(8,128)}, f32[512,512...) custom-call(bf16[2,128,512]{2,1,0:T(8,128)(2,1)} %get-tuple-element.11.layer, ...), custom_call_target="tpu_custom_call" | custom-call | tf_op jit(solution)/shard_map/pallas_call | solution.py:729

commit v6 on v5

--- a/solution.py
+++ b/solution.py
@@ -273,10 +273,11 @@
         m.pool[DQUERY, index] = jnp.sum(inner * f32(keys), axis=0).astype(bf16)
         return inner * f32(query)[None], weights * f32(up)[None]
 
-    def attend_two(step, carry):
-        dkey, dvalue = attend(2 * step)
-        dkey_too, dvalue_too = attend(2 * step + 1)
-        dkey, dvalue = dkey + dkey_too, dvalue + dvalue_too
+    def attend_four(step, carry):
+        dkey, dvalue = attend(4 * step)
+        for index in range(1, 4):
+            dkey_too, dvalue_too = attend(4 * step + index)
+            dkey, dvalue = dkey + dkey_too, dvalue + dvalue_too
 
         @pl.when(step == 0)
         def _():
@@ -290,7 +291,7 @@
 
         return carry
 
-    lax.fori_loop(0, 4, attend_two, 0)
+    lax.fori_loop(0, 2, attend_four, 0)
 
     shared[FIRST_S] = to_sibling(DQUERY - other, FIRST_S)
     m.pool[DKEY] = m.dkey[...].astype(bf16)

time: 66.9 us -> 66.6 us (level)
  no operation moved by 1% of the time
where the time goes in v6:
time: 66.6 us; the launch traced here: 66.5 us
  Pallas kernels  65.9 us (99%)
    pallas_call x1, Pallas kernels, shards(): pl.pallas_call(body, out_shape=outputs + (shape((2, 2, 4, 4, SECOND, 128)...  62.5 us
    pallas_call x1, Pallas kernels, shards(): pl.pallas_call(finish_body, out_shape=outputs + (shape((width, width), fu...  3.37 us

profile of v6, /device:TPU:1, one launch (start us, length us, event | category | flops | bytes accessed | tf_op | source)
XLA Modules:
  0.0 66.5 jit_solution(12537509277589106565)
XLA Ops:
  0.6 62.5 %shard_map.126 = (bf16[2,128,512]{2,1,0:T(8,128)(2,1)}, bf16[2,128,512]{2,1,0:T(8,128)(2,1)}, f32[31,512]{1,0:T(8,128)}, bf16[2,2,4,4,128,128]{5,4,3,2,1,0:T(8,128)(2,1)}) custom-call(bf16[2,128,512]{2,1,0:T(8,128)(2,1)} %refs_0_.1, bf16[2,128,512]{2,1,0:T(8,128)(2,1)} %refs_1_.1, f32[31,512]{1,0:T(8,128)} %refs_2_.1, bf16[512,512]{1,0:T(8,128)(2,1)} %refs_3_.1, ...), custom_call_target="tpu_custom_call" | custom-call | tf_op jit(solution)/shard_map/pallas_call | solution.py:719
  63.1 3.4 %shard_map.127 = (bf16[2,128,512]{2,1,0:T(8,128)(2,1)}, bf16[2,128,512]{2,1,0:T(8,128)(2,1)}, f32[31,512]{1,0:T(8,128)}, f32[512,512]{1,0:T(8,128)}, f32[512,512...) custom-call(bf16[2,128,512]{2,1,0:T(8,128)(2,1)} %get-tuple-element.11.layer, ...), custom_call_target="tpu_custom_call" | custom-call | tf_op jit(solution)/shard_map/pallas_call | solution.py:730
